TPU v7x, 32 devices: a whole 2x2x4 slice. The times are simulated.
32 devices in a mesh: rows: 8 (over z, y), trees: 4 (over x, core).
Axes of the slice: x: 2, y: 2, z: 4, core: 2. Of those that a mesh axis runs over, the one named last changes fastest.
Arguments:
- leaf_index: int32 [128, 65536], P(None, ('rows', 'trees')), may hold values from 0 to 31, as said below
- out_of_bag: bfloat16 [128, 65536], P(None, ('rows', 'trees')), may hold values from 0 to 4, as said below
- labels: int32 [65536], P(('rows', 'trees')), may hold values from 0 to 999
Outputs:
- tallies: float32 [128, 32, 1000], P('trees', 'rows')
- tree_error: float32 [128], P('trees')
- forest_error: float32 [], replicated
Inputs may be any that keep to these rules, and one draw needn't show every extreme that they name: `out_of_bag`: 0 exactly where a row was in a tree's sample, else at least 0.25. `leaf_index`: in each tree, the 2048 rows of one device reach every leaf exactly 2048 // 32 times.
All inputs are finite; a program needn't handle non-finite values.
Results may differ from a plain program's by a relative error of at most 0.0003.
Values sent between devices are 32-bit elements; how exact they have to be, the bound alone decides.
A program may use at most 128 MiB of HBM per device.

v0:
```python
import jax
import jax.numpy as jnp
from jax import lax
from jax.sharding import PartitionSpec as P

CLASSES = 1000
LEAVES = 32


def count_table(leaves, weights, row_labels, n_rows):
    leaf_block_size = LEAVES // n_rows
    leaf_grid = jnp.arange(LEAVES, dtype=jnp.int32).reshape(n_rows, leaf_block_size)
    class_ids = jnp.arange(CLASSES, dtype=jnp.int32)
    class_onehot = (row_labels[:, None] == class_ids[None, :]).astype(jnp.bfloat16)
    placed = jnp.where(
        leaves[None, :, None, :] == leaf_grid[:, None, :, None],
        weights[None, :, None, :],
        jnp.zeros((), jnp.bfloat16),
    )
    count_grid = jnp.einsum(
        "rtlz,zc->rtlc", placed, class_onehot, preferred_element_type=jnp.float32
    )
    return count_grid.reshape(-1, CLASSES)


def per_device(leaf_index, out_of_bag, labels):
    n_rows = lax.axis_size("rows")
    tree_count = lax.axis_size("trees")
    tree_block = leaf_index.shape[0] // tree_count
    leaf_block_slice = LEAVES // n_rows
    ordered = count_table(leaf_index, out_of_bag, labels, n_rows)
    owned_part = lax.psum_scatter(ordered, ("rows", "trees"), scatter_dimension=0, tiled=True)
    tallies = owned_part.reshape(tree_block, leaf_block_slice, CLASSES)
    leaf_total = jnp.sum(tallies, axis=2)
    leaf_top = jnp.max(tallies, axis=2)
    local_wrong = jnp.sum(leaf_total - leaf_top, axis=1)
    local_seen = jnp.sum(leaf_total, axis=1)
    wrong_sum, seen_sum = lax.psum((local_wrong, local_seen), "rows")
    tree_error = wrong_sum / seen_sum
    all_wrong, all_seen = lax.psum((jnp.sum(wrong_sum), jnp.sum(seen_sum)), "trees")
    forest_error = all_wrong / all_seen
    return (tallies, tree_error, forest_error)


def solution(mesh):
    in_specs = (P(None, ("rows", "trees")), P(None, ("rows", "trees")), P(("rows", "trees")))
    out_specs = (P("trees", "rows", None), P("trees"), P())
    return jax.shard_map(
        per_device, mesh=mesh, in_specs=in_specs, out_specs=out_specs, check_vma=False
    )
```

profile of v0, /device:TPU:0, one launch (start us, length us, event | category | flops | bytes accessed | tf_op | source)
XLA Modules:
  0.0 295.7 jit_solution(11543535472191394355)
XLA Ops:
  7.2 0.0 reduce-scatter.2.cloned.1.call-start
  7.2 21.7 %fusion = f32[8,128,4,1000]{1,3,2,0:T(8,128)} fusion(s32[8,4]{1,0:T(8,128)S(1)} %multiply_add_fusion, s32[128,2048]{1,0:T(8,128)} %param.3, bf16[128,2048]{1,0:T(8,128)(2,1)} %param.4, s32[2048]{0:T(1024)} %param.5), kind=kOutput, calls=%fused_computation.1 | convolution fusion | flops 16796041216 | bytes 17965184 | tf_op jit(solution)/shard_map/rtlz,zc->rtlc/dot_general | solution.py:20
  29.0 19.9 %copy.6 = f32[8,128,4,1000]{3,2,1,0:T(4,128)} copy(f32[8,128,4,1000]{1,3,2,0:T(8,128)} %fusion) | data formatting | bytes 32768000 | tf_op jit(solution)/shard_map/rtlz,zc->rtlc/dot_general | solution.py:20
  48.9 19.5 %reshape.31 = f32[4096,1000]{1,0:T(8,128)} reshape(f32[8,128,4,1000]{3,2,1,0:T(4,128)} %copy.6) | data formatting | bytes 32768000 | tf_op jit(solution)/shard_map/reshape | solution.py:23
  68.4 0.0 reduce-scatter.2.cloned.1.call-update
  68.4 185.7 %reduce-scatter.2.cloned.1.call-done = f32[128,1000]{1,0:T(8,128)} async-done(((f32[4096,1000]{1,0:T(8,128)}), f32[128,1000]{1,0:T(8,128)}) %reduce-scatter.2.cloned.1.call-update) | async-done | bytes 512016 | tf_op jit(solution)/shard_map/reduce_scatter | solution.py:32
  254.1 1.2 fusion.9
  255.3 0.1 reduce_max.12
  255.4 0.1 reduce_sum.48
  255.5 0.1 fusion.10
  255.6 20.1 %all-reduce = (f32[32]{0:T(128)S(1)}, f32[32]{0:T(128)S(1)}) all-reduce(f32[32]{0:T(128)S(1)} %get-tuple-element.6, f32[32]{0:T(128)S(1)} %get-tuple-element.5), channel_id=1, replica_groups=mesh['rows'=8,'trees'=4] {'rows'}, use_global_device_ids=true, to_apply=%region_4.5 | all-reduce | flops 64 | bytes 512 | tf_op jit(solution)/shard_map/psum | solution.py:38
  275.7 1.1 fusion.11
  276.8 7.6 %all-reduce.1 = (f32[]{:T(128)}, f32[]{:T(128)}) all-reduce(f32[]{:T(128)} %get-tuple-element.13, f32[]{:T(128)} %get-tuple-element.11), channel_id=1, replica_groups=mesh['rows'=8,'trees'=4] {'trees'}, use_global_device_ids=true, to_apply=%region_8.9 | all-reduce | flops 2 | bytes 16 | tf_op jit(solution)/shard_map/psum | solution.py:40
  285.8 2.0 reshape.32
  (1 shorter events, 0.0 us)
Async XLA Ops:
  7.2 247.0 %reduce-scatter.2.cloned.1.call-start = ((), (), s32[]{:S(2)}) async-start(), calls=%async_computation.1 | async-start | bytes 17301504 | tf_op jit(solution)/shard_map/reduce_scatter | solution.py:32
Sparse Core Ops, SparseCore 0:
  68.5 185.5 reduce-scatter.1
where the time goes:
time: 297 us; the launch traced here: 296 us
  waiting for transfers between devices  186 us (63%)
  local copies, waits for them, and re-layouts  41.6 us (14%)
  blocking collectives  27.7 us (9%)
  matrix products  21.7 us (7%)
  between operations  16.5 us (6%)
    reduce_scatter x1, waiting for transfers between devices, per_device(): lax.psum_scatter(ordered, ('rows', 'trees'), scatter_dimension=0, tiled=T...  186 us
    dot_general x1, matrix products, count_table(): jnp.einsum('rtlz,zc->rtlc', placed, class_onehot, preferred_element_type=...  21.7 us
    psum x1, blocking collectives, per_device(): wrong_sum, seen_sum = lax.psum((local_wrong, local_seen), 'rows')  20.1 us
    dot_general x1, local copies, waits for them, and re-layouts, count_table(): jnp.einsum('rtlz,zc->rtlc', placed, class_onehot, preferred_element_type=...  19.9 us
    reshape x1, local copies, waits for them, and re-layouts, count_table(): return count_grid.reshape(-1, CLASSES)  19.5 us
    psum x1, blocking collectives, per_device(): lax.psum((jnp.sum(wrong_sum), jnp.sum(seen_sum)), 'trees')  7.62 us
  transfers between devices with their start and end apart: 1, of which 1 were waited for; matrix products, arithmetic and copies ran while one was open for 0% of the time, Pallas kernels for 0%

commit v1 on v0

v1 whole, which is shorter than its diff:
```python
import functools

import jax
import jax.numpy as jnp
from jax import lax
from jax.experimental import pallas as pl
from jax.experimental.pallas import tpu as pltpu
from jax.sharding import PartitionSpec as P

CLASSES = 1000
LEAVES = 32
LANES = 128
CHUNK = 256


def nt_dot(a, b):
    return lax.dot_general(a, b, (((1,), (1,)), ((), ())), preferred_element_type=jnp.float32)


def compact_tree(leaf_ref, weight_ref, hi_ref, lo_ref, tri_ref, t, rows, slots):
    leaf = leaf_ref[pl.ds(t, 1), :]
    weight = weight_ref[pl.ds(t, 1), :]
    chunks = rows // CHUNK
    leaf_ids = lax.broadcasted_iota(jnp.int32, (LEAVES, CHUNK), 0)
    masks = [leaf[:, c * CHUNK:(c + 1) * CHUNK] == leaf_ids for c in range(chunks)]
    ones = [jnp.where(m, 1.0, 0.0) for m in masks]
    stacked = jnp.concatenate(ones, axis=0).astype(jnp.bfloat16)
    counts = jnp.dot(stacked, tri_ref[...], preferred_element_type=jnp.float32)
    carry = jnp.zeros((LEAVES, 1), jnp.float32)
    slot_ids = lax.broadcasted_iota(jnp.int32, (slots, CHUNK), 0).astype(jnp.float32)
    placed, slot_hot = [], []
    for c in range(chunks):
        running = counts[c * LEAVES:(c + 1) * LEAVES] + carry
        carry = running[:, CHUNK - 1:]
        rank = jnp.sum(jnp.where(masks[c], running, 0.0), axis=0, keepdims=True) - 1.0
        slot_hot.append(jnp.where(rank == slot_ids, 1.0, 0.0).astype(jnp.bfloat16))
        cols = slice(c * CHUNK, (c + 1) * CHUNK)
        w = jnp.where(masks[c], weight[:, cols], 0.0).astype(jnp.bfloat16)
        one = stacked[c * LEAVES:(c + 1) * LEAVES]
        placed.append(jnp.concatenate([w, one * hi_ref[:, cols], one * lo_ref[:, cols]], axis=0))
    out = nt_dot(jnp.concatenate(placed, axis=1), jnp.concatenate(slot_hot, axis=1))
    classes = out[LEAVES:2 * LEAVES] + out[2 * LEAVES:]
    return jnp.concatenate([out[:LEAVES], classes], axis=1)


def compact_kernel(n_rows, leaf_ref, bag_ref, label_ref, send_ref, weight_ref, hi_ref, lo_ref, tri_ref):
    trees, rows = leaf_ref.shape
    slots = rows // LEAVES
    leaf_block = LEAVES // n_rows
    group = max(8 // leaf_block, 2)
    labels = label_ref[...]
    hi = (labels >> 5) << 5
    hi_ref[...] = jnp.broadcast_to(hi.astype(jnp.float32), (LEAVES, rows)).astype(jnp.bfloat16)
    lo_ref[...] = jnp.broadcast_to((labels - hi).astype(jnp.float32), (LEAVES, rows)).astype(jnp.bfloat16)
    r = lax.broadcasted_iota(jnp.int32, (CHUNK, CHUNK), 0)
    c = lax.broadcasted_iota(jnp.int32, (CHUNK, CHUNK), 1)
    tri_ref[...] = jnp.where(r <= c, 1.0, 0.0).astype(jnp.bfloat16)
    weight_ref[...] = bag_ref[...].astype(jnp.float32)

    def step(i, _):
        parts = [
            compact_tree(leaf_ref, weight_ref, hi_ref, lo_ref, tri_ref, i * group + j, rows, slots)
            for j in range(group)
        ]
        size = group * leaf_block
        for b in range(n_rows):
            tile = jnp.concatenate([p[b * leaf_block:(b + 1) * leaf_block] for p in parts], axis=0)
            send_ref[b, pl.ds(pl.multiple_of(i * size, size), size), :] = tile
        return 0

    lax.fori_loop(0, trees // group, step, 0)


def compact(leaf_index, out_of_bag, labels, n_rows):
    trees, rows = leaf_index.shape
    vmem = pl.BlockSpec(memory_space=pltpu.VMEM)
    return pl.pallas_call(
        functools.partial(compact_kernel, n_rows),
        out_shape=jax.ShapeDtypeStruct((n_rows, trees * (LEAVES // n_rows), LANES), jnp.float32),
        in_specs=[vmem] * 3,
        out_specs=vmem,
        scratch_shapes=[
            pltpu.VMEM((trees, rows), jnp.float32),
            pltpu.VMEM((LEAVES, rows), jnp.bfloat16),
            pltpu.VMEM((LEAVES, rows), jnp.bfloat16),
            pltpu.VMEM((CHUNK, CHUNK), jnp.bfloat16),
        ],
        compiler_params=pltpu.CompilerParams(vmem_limit_bytes=48 << 20),
        name="compact",
    )(leaf_index, out_of_bag, labels.reshape(1, rows))


def tally_kernel(recv_ref, tally_ref):
    sources, cells, _ = recv_ref.shape
    pairs = sources // 2
    high = tally_ref.shape[1]
    low_half = lax.broadcasted_iota(jnp.int32, (pairs, 8, LANES), 2) < LANES // 2
    lo_ids = lax.broadcasted_iota(jnp.int32, (LANES, LANES), 0)
    hi_ids = lax.broadcasted_iota(jnp.int32, (high, LANES), 0)

    def step(i, _):
        block = recv_ref[:, pl.ds(pl.multiple_of(i * 8, 8), 8), :]
        block = block.reshape(pairs, 2, 8, LANES)
        first, second = block[:, 0], block[:, 1]
        turned_first = pltpu.roll(first, LANES // 2, 2)
        turned_second = pltpu.roll(second, LANES // 2, 2)
        weight = jnp.where(low_half, first, turned_second)
        label = jnp.where(low_half, turned_first, second).astype(jnp.int32)
        hi, lo = label >> 7, label & (LANES - 1)
        for j in range(8):
            a, b = [], []
            for p in range(pairs):
                a.append(jnp.where(hi[p, j:j + 1] == hi_ids, weight[p, j:j + 1], 0.0))
                b.append(jnp.where(lo[p, j:j + 1] == lo_ids, 1.0, 0.0).astype(jnp.bfloat16))
            a = jnp.concatenate(a, axis=1).astype(jnp.bfloat16)
            tally_ref[i * 8 + j] = nt_dot(a, jnp.concatenate(b, axis=1))
        return 0

    lax.fori_loop(0, cells // 8, step, 0)


def tally(recv):
    sources, cells, _ = recv.shape
    high = pl.cdiv(CLASSES, LANES)
    vmem = pl.BlockSpec(memory_space=pltpu.VMEM)
    return pl.pallas_call(
        tally_kernel,
        out_shape=jax.ShapeDtypeStruct((cells, high, LANES), jnp.float32),
        in_specs=[vmem],
        out_specs=vmem,
        compiler_params=pltpu.CompilerParams(vmem_limit_bytes=48 << 20),
        name="tally",
    )(recv)


def per_device(leaf_index, out_of_bag, labels):
    n_rows = lax.axis_size("rows")
    tree_count = lax.axis_size("trees")
    trees = leaf_index.shape[0]
    tree_block = trees // tree_count
    leaf_block = LEAVES // n_rows
    cells = tree_block * leaf_block
    send = compact(leaf_index, out_of_bag, labels, n_rows)
    send = send.reshape(n_rows * tree_count, cells, LANES)
    recv = lax.all_to_all(send, ("rows", "trees"), split_axis=0, concat_axis=0, tiled=True)
    table = tally(recv).reshape(cells, -1)
    tallies = table[:, :CLASSES].reshape(tree_block, leaf_block, CLASSES)
    leaf_total = jnp.sum(tallies, axis=2)
    leaf_top = jnp.max(tallies, axis=2)
    local = jnp.stack([jnp.sum(leaf_total - leaf_top, axis=1), jnp.sum(leaf_total, axis=1)])
    mine = lax.axis_index("trees") * tree_block
    spread = lax.dynamic_update_slice(jnp.zeros((2, trees), jnp.float32), local, (0, mine))
    sums = lax.psum(spread, ("rows", "trees"))
    own = lax.dynamic_slice(sums, (0, mine), (2, tree_block))
    tree_error = own[0] / own[1]
    pooled = jnp.sum(sums, axis=1)
    return tallies, tree_error, pooled[0] / pooled[1]


def solution(mesh):
    in_specs = (P(None, ("rows", "trees")), P(None, ("rows", "trees")), P(("rows", "trees")))
    out_specs = (P("trees", "rows", None), P("trees"), P())
    return jax.shard_map(
        per_device, mesh=mesh, in_specs=in_specs, out_specs=out_specs, check_vma=False
    )
```

time: 297 us -> 183 us (0.62)
  waiting for transfers between devices: 186 us -> 48.9 us
  Pallas kernels: 0 us -> 77.3 us
  local copies, waits for them, and re-layouts: 41.6 us -> 6.37 us
  matrix products: 21.7 us -> 0 us
  between operations: 16.5 us -> 3.23 us
  blocking collectives: 27.7 us -> 38.2 us
  starting transfers between devices: 0.04 us -> 7.29 us
    reduce_scatter x1 -> x0, waiting for transfers between devices: 186 us -> none  [per_device(): lax.psum_scatter(ordered, ('rows', 'trees'), scatter_dimension=0, tiled=T...]
    pallas_call x0 -> x2, Pallas kernels: none -> 77.3 us  [the longest x1 56.9 us: compact(): pl.pallas_call(functools.partial(compact_kernel, n_rows), out_shape=jax.S...]
    all_to_all x0 -> x1, waiting for transfers between devices: none -> 48.9 us  [per_device(): lax.all_to_all(send, ('rows', 'trees'), split_axis=0, concat_axis=0, tile...]
    dot_general x1 -> x0, matrix products: 21.7 us -> none  [count_table(): jnp.einsum('rtlz,zc->rtlc', placed, class_onehot, preferred_element_type=...]
    reshape x2 -> x1, local copies, waits for them, and re-layouts: 21.5 us -> 0.95 us  [per_device(): tallies = table[:, :CLASSES].reshape(tree_block, leaf_block, CLASSES)]
    dot_general x1 -> x0, local copies, waits for them, and re-layouts: 19.9 us -> none  [count_table(): jnp.einsum('rtlz,zc->rtlc', placed, class_onehot, preferred_element_type=...]
    psum x2 -> x1, blocking collectives: 27.7 us -> 38.2 us  [per_device(): sums = lax.psum(spread, ('rows', 'trees'))]
    all_to_all x0 -> x1, starting transfers between devices: none -> 7.29 us  [per_device(): lax.all_to_all(send, ('rows', 'trees'), split_axis=0, concat_axis=0, tile...]
where the time goes in v1:
time: 183 us; the launch traced here: 182 us
  Pallas kernels  77.3 us (42%)
  waiting for transfers between devices  48.9 us (27%)
  blocking collectives  38.2 us (21%)
  starting transfers between devices  7.29 us (4%)
  local copies, waits for them, and re-layouts  6.37 us (3%)
  between operations  3.23 us (2%)
    pallas_call x1, Pallas kernels, compact(): pl.pallas_call(functools.partial(compact_kernel, n_rows), out_shape=jax.S...  56.9 us
    all_to_all x1, waiting for transfers between devices, per_device(): lax.all_to_all(send, ('rows', 'trees'), split_axis=0, concat_axis=0, tile...  48.9 us
    psum x1, blocking collectives, per_device(): sums = lax.psum(spread, ('rows', 'trees'))  38.2 us
    pallas_call x1, Pallas kernels, tally(): pl.pallas_call(tally_kernel, out_shape=jax.ShapeDtypeStruct((cells, high,...  20.4 us
    all_to_all x1, starting transfers between devices, per_device(): lax.all_to_all(send, ('rows', 'trees'), split_axis=0, concat_axis=0, tile...  7.29 us
    unnamed x9, local copies, waits for them, and re-layouts  4.41 us
  transfers between devices with their start and end apart: 1, of which 1 were waited for; matrix products, arithmetic and copies ran while one was open for 0% of the time, Pallas kernels for 0%

profile of v1, /device:TPU:0, one launch (start us, length us, event | category | flops | bytes accessed | tf_op | source)
XLA Modules:
  0.0 182.1 jit_solution(7945155398035064911)
XLA Ops:
  0.6 0.0 copy-start.1
  0.6 1.2 copy-done.1
  1.9 0.0 copy-start.2
  1.9 1.0 copy-done.2
  2.9 0.0 copy-start.3
  2.9 0.7 copy-done.3
  3.6 56.9 %compact.1 = f32[8,512,128]{2,1,0:T(8,128)S(1)} custom-call(s32[128,2048]{1,0:T(8,128)S(1)} %copy-done.1, bf16[128,2048]{1,0:T(8,128)(2,1)S(1)} %copy-done.2, s32[1,2048]{1,0:T(1,128)S(1)} %bitcast.13), custom_call_target="tpu_custom_call" | custom-call | tf_op jit(solution)/shard_map/compact/pallas_call | solution.py:77
  60.5 0.0 copy-start
  60.5 1.3 copy-done
  61.9 7.3 %all-to-all-start = ((f32[32,128,128]{2,1,0:T(8,128)}), f32[32,128,128]{2,1,0:T(8,128)S(1)}, u32[]{:S(2)}, u32[]{:S(2)}) async-start(f32[32,128,128]{2,1,0:T(8,128)} %bitcast.11), calls=%async_computation | async-start | bytes 4194304 | tf_op jit(solution)/shard_map/all_to_all | solution.py:145
  69.2 48.9 %all-to-all-done.recv_ref = f32[32,128,128]{2,1,0:T(8,128)S(1)} async-done(((f32[32,128,128]{2,1,0:T(8,128)}), f32[32,128,128]{2,1,0:T(8,128)S(1)}, u32[]{:S(2)}, u32[]{:S(2)}) %all-to-all-start) | async-done | bytes 2097184 | tf_op jit(solution)/shard_map/all_to_all | solution.py:145
  118.1 20.4 %tally.1 = f32[128,8,128]{2,1,0:T(8,128)S(1)} custom-call(f32[32,128,128]{2,1,0:T(8,128)S(1)} %all-to-all-done.recv_ref), custom_call_target="tpu_custom_call" | custom-call | tf_op jit(solution)/shard_map/tally/pallas_call | solution.py:126
  138.4 0.1 copy.8
  138.6 0.1 slice_reduce_fusion
  138.7 0.1 reduce_max.12
  138.8 0.1 reduce_sum.39
  138.9 0.1 subtract_reduce_fusion
  139.0 0.1 dynamic_update_slice.3
  139.2 38.2 %psum.7 = f32[2,128]{1,0:T(2,128)S(1)} all-reduce(f32[2,128]{1,0:T(2,128)S(1)} %dynamic_update_slice.3), channel_id=1, replica_groups=mesh['rows'=8,'trees'=4] {'rows','trees'}, use_global_device_ids=true, to_apply=%region_4.0 | all-reduce | flops 256 | bytes 2048 | tf_op jit(solution)/shard_map/psum | solution.py:153
  177.4 0.1 reduce_sum.42
  177.5 0.1 constant_dynamic-slice_fusion
  177.6 0.6 fusion.1
  178.2 0.5 fusion
  178.7 0.9 reshape.26
  (2 shorter events, 0.0 us)
Async XLA Ops:
  0.6 1.2 copy-start.1
  1.9 1.0 copy-start.2
  2.9 0.7 copy-start.3
  60.5 1.4 copy-start
  61.9 56.2 %all-to-all-start = ((f32[32,128,128]{2,1,0:T(8,128)}), f32[32,128,128]{2,1,0:T(8,128)S(1)}, u32[]{:S(2)}, u32[]{:S(2)}) async-start(f32[32,128,128]{2,1,0:T(8,128)} %bitcast.11), calls=%async_computation | async-start | bytes 4194304 | tf_op jit(solution)/shard_map/all_to_all | solution.py:145

commit v2 on v1

--- a/solution.py
+++ b/solution.py
@@ -43,11 +43,36 @@
     return jnp.concatenate([out[:LEAVES], classes], axis=1)
 
 
-def compact_kernel(n_rows, leaf_ref, bag_ref, label_ref, send_ref, weight_ref, hi_ref, lo_ref, tri_ref):
+def others(n, me, body):
+    lax.fori_loop(1, n, lambda k, _: body(lax.rem(me + k, n)) or 0, 0)
+
+
+def greet_all(n, tree_count, me):
+    barrier = pltpu.get_barrier_semaphore()
+
+    def greet(other):
+        pl.semaphore_signal(
+            barrier, inc=1, device_id=(other // tree_count, lax.rem(other, tree_count)),
+            device_id_type=pl.DeviceIdType.MESH,
+        )
+
+    others(n, me, greet)
+    return lambda: pl.semaphore_wait(barrier, n - 1)
+
+
+def compact_kernel(n_rows, tree_count, leaf_ref, bag_ref, label_ref, recv_ref, send_ref, weight_ref,
+                   hi_ref, lo_ref, tri_ref, send_sem, recv_sem, own_sem):
     trees, rows = leaf_ref.shape
     slots = rows // LEAVES
     leaf_block = LEAVES // n_rows
     group = max(8 // leaf_block, 2)
+    size = group * leaf_block
+    tree_block = trees // tree_count
+    n = n_rows * tree_count
+    my_row, my_tree = lax.axis_index("rows"), lax.axis_index("trees")
+    me = my_row * tree_count + my_tree
+    wait_all = greet_all(n, tree_count, me)
+
     labels = label_ref[...]
     hi = (labels >> 5) << 5
     hi_ref[...] = jnp.broadcast_to(hi.astype(jnp.float32), (LEAVES, rows)).astype(jnp.bfloat16)
@@ -57,40 +82,128 @@
     tri_ref[...] = jnp.where(r <= c, 1.0, 0.0).astype(jnp.bfloat16)
     weight_ref[...] = bag_ref[...].astype(jnp.float32)
 
-    def step(i, _):
-        parts = [
-            compact_tree(leaf_ref, weight_ref, hi_ref, lo_ref, tri_ref, i * group + j, rows, slots)
-            for j in range(group)
-        ]
-        size = group * leaf_block
-        for b in range(n_rows):
-            tile = jnp.concatenate([p[b * leaf_block:(b + 1) * leaf_block] for p in parts], axis=0)
-            send_ref[b, pl.ds(pl.multiple_of(i * size, size), size), :] = tile
+    def transfer(block, slot, other):
+        return pltpu.make_async_remote_copy(
+            src_ref=send_ref.at[block],
+            dst_ref=recv_ref.at[slot],
+            send_sem=send_sem.at[block],
+            recv_sem=recv_sem.at[slot],
+            device_id=(other // tree_count, lax.rem(other, tree_count)),
+            device_id_type=pl.DeviceIdType.MESH,
+        )
+
+    def phase(tt):
+        def step(i, _):
+            parts = [
+                compact_tree(leaf_ref, weight_ref, hi_ref, lo_ref, tri_ref,
+                             tt * tree_block + i * group + j, rows, slots)
+                for j in range(group)
+            ]
+            for b in range(n_rows):
+                tile = jnp.concatenate([p[b * leaf_block:(b + 1) * leaf_block] for p in parts], axis=0)
+                send_ref[b * tree_count + tt, pl.ds(pl.multiple_of(i * size, size), size), :] = tile
+            return 0
+
+        lax.fori_loop(0, tree_block // group, step, 0)
+
+    def send(k, tt):
+        other = lax.rem(my_row + k, n_rows) * tree_count + tt
+        transfer(other, me, other).start()
+
+    def away(i, _):
+        tt = lax.rem(my_tree + i, tree_count)
+        phase(tt)
+        lax.fori_loop(0, n_rows, lambda k, _: send(k, tt) or 0, 0)
         return 0
 
-    lax.fori_loop(0, trees // group, step, 0)
-
-
-def compact(leaf_index, out_of_bag, labels, n_rows):
+    wait_all()
+    lax.fori_loop(1, tree_count, away, 0)
+    phase(my_tree)
+    lax.fori_loop(1, n_rows, lambda k, _: send(k, my_tree) or 0, 0)
+    own = pltpu.make_async_copy(send_ref.at[me], recv_ref.at[me], own_sem)
+    own.start()
+    others(n, me, lambda other: transfer(other, other, other).wait())
+    own.wait()
+
+
+def compact(leaf_index, out_of_bag, labels, n_rows, tree_count):
     trees, rows = leaf_index.shape
+    n = n_rows * tree_count
+    cells = (trees // tree_count) * (LEAVES // n_rows)
     vmem = pl.BlockSpec(memory_space=pltpu.VMEM)
     return pl.pallas_call(
-        functools.partial(compact_kernel, n_rows),
-        out_shape=jax.ShapeDtypeStruct((n_rows, trees * (LEAVES // n_rows), LANES), jnp.float32),
+        functools.partial(compact_kernel, n_rows, tree_count),
+        out_shape=jax.ShapeDtypeStruct((n, cells, LANES), jnp.float32),
         in_specs=[vmem] * 3,
-        out_specs=vmem,
+        out_specs=pl.BlockSpec(memory_space=pl.ANY),
         scratch_shapes=[
+            pltpu.VMEM((n, cells, LANES), jnp.float32),
             pltpu.VMEM((trees, rows), jnp.float32),
             pltpu.VMEM((LEAVES, rows), jnp.bfloat16),
             pltpu.VMEM((LEAVES, rows), jnp.bfloat16),
             pltpu.VMEM((CHUNK, CHUNK), jnp.bfloat16),
+            pltpu.SemaphoreType.DMA((n,)),
+            pltpu.SemaphoreType.DMA((n,)),
+            pltpu.SemaphoreType.DMA,
         ],
-        compiler_params=pltpu.CompilerParams(vmem_limit_bytes=48 << 20),
+        compiler_params=pltpu.CompilerParams(
+            vmem_limit_bytes=48 << 20, collective_id=0, has_side_effects=True
+        ),
         name="compact",
     )(leaf_index, out_of_bag, labels.reshape(1, rows))
 
 
-def tally_kernel(recv_ref, tally_ref):
+def rates_kernel(n_rows, tree_count, local_ref, out_ref, recv_ref, send_sem, recv_sem):
+    n = n_rows * tree_count
+    my_row, my_tree = lax.axis_index("rows"), lax.axis_index("trees")
+    me = my_row * tree_count + my_tree
+    wait_all = greet_all(n, tree_count, me)
+    wait_all()
+
+    def transfer(slot, other):
+        return pltpu.make_async_remote_copy(
+            src_ref=local_ref,
+            dst_ref=recv_ref.at[slot],
+            send_sem=send_sem.at[other],
+            recv_sem=recv_sem.at[slot],
+            device_id=(other // tree_count, lax.rem(other, tree_count)),
+            device_id_type=pl.DeviceIdType.MESH,
+        )
+
+    others(n, me, lambda other: transfer(me, other).start())
+    recv_ref[me] = local_ref[...]
+    others(n, me, lambda other: transfer(other, other).wait())
+    mine = jnp.zeros((8, LANES), jnp.float32)
+    total = jnp.zeros((8, LANES), jnp.float32)
+    for row in range(n_rows):
+        mine += recv_ref[row * tree_count + my_tree]
+    for device in range(n):
+        total += recv_ref[device]
+    pooled = jnp.sum(total, axis=1, keepdims=True)
+    out_ref[0:1] = mine[0:1] / jnp.where(mine[2:3] > 0, mine[1:2], 1.0)
+    out_ref[1:2] = jnp.broadcast_to(pooled[0:1] / pooled[1:2], (1, LANES))
+    out_ref[2:] = jnp.zeros((6, LANES), jnp.float32)
+
+
+def rates(local, n_rows, tree_count):
+    n = n_rows * tree_count
+    vmem = pl.BlockSpec(memory_space=pltpu.VMEM)
+    return pl.pallas_call(
+        functools.partial(rates_kernel, n_rows, tree_count),
+        out_shape=jax.ShapeDtypeStruct((8, LANES), jnp.float32),
+        in_specs=[vmem],
+        out_specs=vmem,
+        scratch_shapes=[
+            pltpu.VMEM((n, 8, LANES), jnp.float32),
+            pltpu.SemaphoreType.DMA((n,)),
+            pltpu.SemaphoreType.DMA((n,)),
+        ],
+        compiler_params=pltpu.CompilerParams(collective_id=1, has_side_effects=True),
+        name="rates",
+    )(local)
+
+
+def tally_kernel(leaf_block, recv_ref, tally_ref, sums_ref):
     sources, cells, _ = recv_ref.shape
     pairs = sources // 2
     high = tally_ref.shape[1]
@@ -117,17 +230,29 @@
         return 0
 
     lax.fori_loop(0, cells // 8, step, 0)
-
-
-def tally(recv):
+    table = tally_ref[...]
+    seen = jnp.sum(jnp.sum(table, axis=1), axis=1, keepdims=True)
+    top = jnp.max(jnp.max(table, axis=1), axis=1, keepdims=True)
+    tree = lax.broadcasted_iota(jnp.int32, (cells, LANES), 0) // leaf_block
+    held = tree == lax.broadcasted_iota(jnp.int32, (cells, LANES), 1)
+    sums_ref[...] = jnp.zeros((8, LANES), jnp.float32)
+    sums_ref[0:1] = jnp.sum(jnp.where(held, seen - top, 0.0), axis=0, keepdims=True)
+    sums_ref[1:2] = jnp.sum(jnp.where(held, seen, 0.0), axis=0, keepdims=True)
+    sums_ref[2:3] = jnp.sum(jnp.where(held, 1.0, 0.0), axis=0, keepdims=True)
+
+
+def tally(recv, leaf_block):
     sources, cells, _ = recv.shape
     high = pl.cdiv(CLASSES, LANES)
     vmem = pl.BlockSpec(memory_space=pltpu.VMEM)
     return pl.pallas_call(
-        tally_kernel,
-        out_shape=jax.ShapeDtypeStruct((cells, high, LANES), jnp.float32),
+        functools.partial(tally_kernel, leaf_block),
+        out_shape=[
+            jax.ShapeDtypeStruct((cells, high, LANES), jnp.float32),
+            jax.ShapeDtypeStruct((8, LANES), jnp.float32),
+        ],
         in_specs=[vmem],
-        out_specs=vmem,
+        out_specs=[vmem, vmem],
         compiler_params=pltpu.CompilerParams(vmem_limit_bytes=48 << 20),
         name="tally",
     )(recv)
@@ -140,21 +265,11 @@
     tree_block = trees // tree_count
     leaf_block = LEAVES // n_rows
     cells = tree_block * leaf_block
-    send = compact(leaf_index, out_of_bag, labels, n_rows)
-    send = send.reshape(n_rows * tree_count, cells, LANES)
-    recv = lax.all_to_all(send, ("rows", "trees"), split_axis=0, concat_axis=0, tiled=True)
-    table = tally(recv).reshape(cells, -1)
-    tallies = table[:, :CLASSES].reshape(tree_block, leaf_block, CLASSES)
-    leaf_total = jnp.sum(tallies, axis=2)
-    leaf_top = jnp.max(tallies, axis=2)
-    local = jnp.stack([jnp.sum(leaf_total - leaf_top, axis=1), jnp.sum(leaf_total, axis=1)])
-    mine = lax.axis_index("trees") * tree_block
-    spread = lax.dynamic_update_slice(jnp.zeros((2, trees), jnp.float32), local, (0, mine))
-    sums = lax.psum(spread, ("rows", "trees"))
-    own = lax.dynamic_slice(sums, (0, mine), (2, tree_block))
-    tree_error = own[0] / own[1]
-    pooled = jnp.sum(sums, axis=1)
-    return tallies, tree_error, pooled[0] / pooled[1]
+    recv = compact(leaf_index, out_of_bag, labels, n_rows, tree_count)
+    table, sums = tally(recv, leaf_block)
+    tallies = table.reshape(cells, -1)[:, :CLASSES].reshape(tree_block, leaf_block, CLASSES)
+    result = rates(sums, n_rows, tree_count)
+    return tallies, result[0, :tree_block], result[1, 0]
 
 
 def solution(mesh):

time: 183 us -> 116 us (0.63)
  waiting for transfers between devices: 48.9 us -> 0 us
  blocking collectives: 38.2 us -> 0 us
  Pallas kernels: 77.3 us -> 108 us
  starting transfers between devices: 7.29 us -> 0 us
  between operations: 3.23 us -> 0.68 us
    all_to_all x1 -> x0, waiting for transfers between devices: 48.9 us -> none  [per_device(): lax.all_to_all(send, ('rows', 'trees'), split_axis=0, concat_axis=0, tile...]
    psum x1 -> x0, blocking collectives: 38.2 us -> none  [per_device(): sums = lax.psum(spread, ('rows', 'trees'))]
    pallas_call x2 -> x3, Pallas kernels: 77.3 us -> 108 us  [the longest x1 73.8 us: compact(): pl.pallas_call(functools.partial(compact_kernel, n_rows, tree_count), out...]
    all_to_all x1 -> x0, starting transfers between devices: 7.29 us -> none  [per_device(): lax.all_to_all(send, ('rows', 'trees'), split_axis=0, concat_axis=0, tile...]
  transfers between devices with their start and end apart: 1 -> 0, of which waited for: 1 -> 0; matrix products, arithmetic and copies ran while one was open for 0% -> 0% of each run, Pallas kernels for 0% -> 0%
where the time goes in v2:
time: 116 us; the launch traced here: 115 us
  Pallas kernels  108 us (93%)
  local copies, waits for them, and re-layouts  6.89 us (6%)
    pallas_call x1, Pallas kernels, compact(): pl.pallas_call(functools.partial(compact_kernel, n_rows, tree_count), out...  73.8 us
    pallas_call x1, Pallas kernels, tally(): pl.pallas_call(functools.partial(tally_kernel, leaf_block), out_shape=[ja...  20.7 us
    pallas_call x1, Pallas kernels, rates(): pl.pallas_call(functools.partial(rates_kernel, n_rows, tree_count), out_s...  13.3 us
    unnamed x9, local copies, waits for them, and re-layouts  3.55 us

profile of v2, /device:TPU:0, one launch (start us, length us, event | category | flops | bytes accessed | tf_op | source)
XLA Modules:
  0.0 115.3 jit_solution(1450723852614547129)
XLA Ops:
  0.6 0.0 copy-start
  0.6 1.2 %copy-done = s32[128,2048]{1,0:T(8,128)S(1)} copy-done((s32[128,2048]{1,0:T(8,128)S(1)}, s32[128,2048]{1,0:T(8,128)}, u32[]{:S(2)}) %copy-start) | copy-done | bytes 1048600
  1.9 0.0 copy-start.1
  1.9 1.0 copy-done.1
  2.9 0.0 copy-start.2
  2.9 0.7 copy-done.2
  3.6 73.8 %compact.1.recv_ref = f32[32,128,128]{2,1,0:T(8,128)S(1)} custom-call(s32[128,2048]{1,0:T(8,128)S(1)} %copy-done, bf16[128,2048]{1,0:T(8,128)(2,1)S(1)} %copy-done.1, s32[1,2048]{1,0:T(1,128)S(1)} %bitcast.10), custom_call_target="tpu_custom_call" | custom-call | tf_op jit(solution)/shard_map/compact/pallas_call | solution.py:134
  77.4 20.7 %tally.1 = (f32[128,8,128]{2,1,0:T(8,128)S(1)}, f32[8,128]{1,0:T(8,128)S(1)}) custom-call(f32[32,128,128]{2,1,0:T(8,128)S(1)} %compact.1.recv_ref), custom_call_target="tpu_custom_call" | custom-call | tf_op jit(solution)/shard_map/tally/pallas_call | solution.py:248
  98.1 0.0 copy-start.3
  98.1 0.1 copy.8
  98.2 0.5 copy-done.3
  98.7 0.9 reshape.17
  99.6 13.3 %rates.1 = f32[8,128]{1,0:T(8,128)} custom-call(f32[8,128]{1,0:T(8,128)} %copy-done.3), custom_call_target="tpu_custom_call" | custom-call | tf_op jit(solution)/shard_map/rates/pallas_call | solution.py:191
  112.9 1.2 %slice.11 = f32[1,1]{1,0:T(1,128)} slice(f32[8,128]{1,0:T(8,128)} %rates.1), slice={[1:2], [0:1]} | slice | bytes 8 | tf_op jit(solution)/shard_map/slice | solution.py:272
  114.1 1.2 %slice_bitcast_fusion = f32[32]{0:T(128)} fusion(f32[8,128]{1,0:T(8,128)} %rates.1), kind=kLoop, calls=%fused_computation.1 | loop fusion | bytes 256 | tf_op jit(solution)/shard_map/squeeze | solution.py:272
Async XLA Ops:
  0.6 1.2 %copy-start = (s32[128,2048]{1,0:T(8,128)S(1)}, s32[128,2048]{1,0:T(8,128)}, u32[]{:S(2)}) copy-start(s32[128,2048]{1,0:T(8,128)} %leaf_ref.1) | copy-start | bytes 3145732
  1.9 1.0 copy-start.1
  2.9 0.7 copy-start.2
  98.1 0.6 copy-start.3

commit v3 on v2

--- a/solution.py
+++ b/solution.py
@@ -11,36 +11,61 @@
 LEAVES = 32
 LANES = 128
 CHUNK = 256
+GROUP = 4
 
 
 def nt_dot(a, b):
     return lax.dot_general(a, b, (((1,), (1,)), ((), ())), preferred_element_type=jnp.float32)
 
 
-def compact_tree(leaf_ref, weight_ref, hi_ref, lo_ref, tri_ref, t, rows, slots):
-    leaf = leaf_ref[pl.ds(t, 1), :]
-    weight = weight_ref[pl.ds(t, 1), :]
+def rows16(row):
+    return jnp.broadcast_to(row, (16, row.shape[1])).astype(jnp.bfloat16)
+
+
+def ids16(first, width):
+    return (lax.broadcasted_iota(jnp.int32, (16, width), 0) + first).astype(jnp.float32).astype(jnp.bfloat16)
+
+
+def compact_group(group, leaf_ref, weight_ref, hi_ref, lo_ref, tri_ref, mask_ref, hot_ref, placed_ref, first, slots):
+    rows = leaf_ref.shape[1]
     chunks = rows // CHUNK
-    leaf_ids = lax.broadcasted_iota(jnp.int32, (LEAVES, CHUNK), 0)
-    masks = [leaf[:, c * CHUNK:(c + 1) * CHUNK] == leaf_ids for c in range(chunks)]
-    ones = [jnp.where(m, 1.0, 0.0) for m in masks]
-    stacked = jnp.concatenate(ones, axis=0).astype(jnp.bfloat16)
-    counts = jnp.dot(stacked, tri_ref[...], preferred_element_type=jnp.float32)
-    carry = jnp.zeros((LEAVES, 1), jnp.float32)
-    slot_ids = lax.broadcasted_iota(jnp.int32, (slots, CHUNK), 0).astype(jnp.float32)
-    placed, slot_hot = [], []
-    for c in range(chunks):
-        running = counts[c * LEAVES:(c + 1) * LEAVES] + carry
-        carry = running[:, CHUNK - 1:]
-        rank = jnp.sum(jnp.where(masks[c], running, 0.0), axis=0, keepdims=True) - 1.0
-        slot_hot.append(jnp.where(rank == slot_ids, 1.0, 0.0).astype(jnp.bfloat16))
-        cols = slice(c * CHUNK, (c + 1) * CHUNK)
-        w = jnp.where(masks[c], weight[:, cols], 0.0).astype(jnp.bfloat16)
-        one = stacked[c * LEAVES:(c + 1) * LEAVES]
-        placed.append(jnp.concatenate([w, one * hi_ref[:, cols], one * lo_ref[:, cols]], axis=0))
-    out = nt_dot(jnp.concatenate(placed, axis=1), jnp.concatenate(slot_hot, axis=1))
-    classes = out[LEAVES:2 * LEAVES] + out[2 * LEAVES:]
-    return jnp.concatenate([out[:LEAVES], classes], axis=1)
+    one, zero = jnp.ones((), jnp.bfloat16), jnp.zeros((), jnp.bfloat16)
+    leaf_ids = [ids16(q * 16, CHUNK) for q in range(LEAVES // 16)]
+    slot_ids = [ids16(q * 16, CHUNK) for q in range(slots // 16)]
+    leaf_ids32 = lax.broadcasted_iota(jnp.int32, (LEAVES, CHUNK), 0)
+    for j in range(group):
+        for c in range(chunks):
+            cols = slice(c * CHUNK, (c + 1) * CHUNK)
+            leaf = rows16(leaf_ref[pl.ds(first + j, 1), cols].astype(jnp.float32))
+            weight = rows16(weight_ref[pl.ds(first + j, 1), cols])
+            for q in range(LEAVES // 16):
+                mask = leaf == leaf_ids[q]
+                at = (j * chunks + c) * LEAVES + q * 16
+                mask_ref[at:at + 16, :] = jnp.where(mask, one, zero)
+                at = j * 3 * LEAVES + q * 16
+                placed_ref[at:at + 16, cols] = jnp.where(mask, weight, zero)
+                placed_ref[at + LEAVES:at + LEAVES + 16, cols] = jnp.where(mask, hi_ref[:, cols], zero)
+                placed_ref[at + 2 * LEAVES:at + 2 * LEAVES + 16, cols] = jnp.where(mask, lo_ref[:, cols], zero)
+    counts = jnp.dot(mask_ref[...], tri_ref[...], preferred_element_type=jnp.float32)
+    for j in range(group):
+        carry = jnp.zeros((LEAVES, 1), jnp.float32)
+        for c in range(chunks):
+            cols = slice(c * CHUNK, (c + 1) * CHUNK)
+            at = (j * chunks + c) * LEAVES
+            running = counts[at:at + LEAVES] + carry
+            carry = running[:, CHUNK - 1:]
+            mask = leaf_ref[pl.ds(first + j, 1), cols] == leaf_ids32
+            rank = rows16(jnp.sum(jnp.where(mask, running, 0.0), axis=0, keepdims=True) - 1.0)
+            for q in range(slots // 16):
+                at = j * slots + q * 16
+                hot_ref[at:at + 16, cols] = jnp.where(rank == slot_ids[q], one, zero)
+    out = nt_dot(placed_ref[...], hot_ref[...])
+    parts = []
+    for j in range(group):
+        mine = out[j * 3 * LEAVES:(j + 1) * 3 * LEAVES, j * slots:(j + 1) * slots]
+        classes = mine[LEAVES:2 * LEAVES] + mine[2 * LEAVES:]
+        parts.append(jnp.concatenate([mine[:LEAVES], classes], axis=1))
+    return parts
 
 
 def others(n, me, body):
@@ -61,11 +86,11 @@
 
 
 def compact_kernel(n_rows, tree_count, leaf_ref, bag_ref, label_ref, recv_ref, send_ref, weight_ref,
-                   hi_ref, lo_ref, tri_ref, send_sem, recv_sem, own_sem):
+                   hi_ref, lo_ref, tri_ref, mask_ref, hot_ref, placed_ref, send_sem, recv_sem, own_sem):
     trees, rows = leaf_ref.shape
     slots = rows // LEAVES
     leaf_block = LEAVES // n_rows
-    group = max(8 // leaf_block, 2)
+    group = GROUP
     size = group * leaf_block
     tree_block = trees // tree_count
     n = n_rows * tree_count
@@ -75,8 +100,8 @@
 
     labels = label_ref[...]
     hi = (labels >> 5) << 5
-    hi_ref[...] = jnp.broadcast_to(hi.astype(jnp.float32), (LEAVES, rows)).astype(jnp.bfloat16)
-    lo_ref[...] = jnp.broadcast_to((labels - hi).astype(jnp.float32), (LEAVES, rows)).astype(jnp.bfloat16)
+    hi_ref[...] = rows16(hi.astype(jnp.float32))
+    lo_ref[...] = rows16((labels - hi).astype(jnp.float32))
     r = lax.broadcasted_iota(jnp.int32, (CHUNK, CHUNK), 0)
     c = lax.broadcasted_iota(jnp.int32, (CHUNK, CHUNK), 1)
     tri_ref[...] = jnp.where(r <= c, 1.0, 0.0).astype(jnp.bfloat16)
@@ -94,11 +119,8 @@
 
     def phase(tt):
         def step(i, _):
-            parts = [
-                compact_tree(leaf_ref, weight_ref, hi_ref, lo_ref, tri_ref,
-                             tt * tree_block + i * group + j, rows, slots)
-                for j in range(group)
-            ]
+            parts = compact_group(group, leaf_ref, weight_ref, hi_ref, lo_ref, tri_ref, mask_ref, hot_ref,
+                                  placed_ref, tt * tree_block + i * group, slots)
             for b in range(n_rows):
                 tile = jnp.concatenate([p[b * leaf_block:(b + 1) * leaf_block] for p in parts], axis=0)
                 send_ref[b * tree_count + tt, pl.ds(pl.multiple_of(i * size, size), size), :] = tile
@@ -139,9 +161,12 @@
         scratch_shapes=[
             pltpu.VMEM((n, cells, LANES), jnp.float32),
             pltpu.VMEM((trees, rows), jnp.float32),
-            pltpu.VMEM((LEAVES, rows), jnp.bfloat16),
-            pltpu.VMEM((LEAVES, rows), jnp.bfloat16),
+            pltpu.VMEM((16, rows), jnp.bfloat16),
+            pltpu.VMEM((16, rows), jnp.bfloat16),
             pltpu.VMEM((CHUNK, CHUNK), jnp.bfloat16),
+            pltpu.VMEM((GROUP * LEAVES * (rows // CHUNK), CHUNK), jnp.bfloat16),
+            pltpu.VMEM((GROUP * (rows // LEAVES), rows), jnp.bfloat16),
+            pltpu.VMEM((GROUP * 3 * LEAVES, rows), jnp.bfloat16),
             pltpu.SemaphoreType.DMA((n,)),
             pltpu.SemaphoreType.DMA((n,)),
             pltpu.SemaphoreType.DMA,
@@ -206,10 +231,11 @@
 def tally_kernel(leaf_block, recv_ref, tally_ref, sums_ref):
     sources, cells, _ = recv_ref.shape
     pairs = sources // 2
-    high = tally_ref.shape[1]
     low_half = lax.broadcasted_iota(jnp.int32, (pairs, 8, LANES), 2) < LANES // 2
-    lo_ids = lax.broadcasted_iota(jnp.int32, (LANES, LANES), 0)
-    hi_ids = lax.broadcasted_iota(jnp.int32, (high, LANES), 0)
+    half = LANES // 2
+    lo_ids = [ids16(q * 16, LANES) for q in range(half // 16)]
+    hi_ids = ids16(0, LANES)
+    one, zero = jnp.ones((), jnp.bfloat16), jnp.zeros((), jnp.bfloat16)
 
     def step(i, _):
         block = recv_ref[:, pl.ds(pl.multiple_of(i * 8, 8), 8), :]
@@ -219,14 +245,16 @@
         turned_second = pltpu.roll(second, LANES // 2, 2)
         weight = jnp.where(low_half, first, turned_second)
         label = jnp.where(low_half, turned_first, second).astype(jnp.int32)
-        hi, lo = label >> 7, label & (LANES - 1)
+        lo = (label & (half - 1)).astype(jnp.float32)
+        hi = ((label >> 7) + ((label >> 6) & 1) * 8).astype(jnp.float32)
         for j in range(8):
             a, b = [], []
             for p in range(pairs):
-                a.append(jnp.where(hi[p, j:j + 1] == hi_ids, weight[p, j:j + 1], 0.0))
-                b.append(jnp.where(lo[p, j:j + 1] == lo_ids, 1.0, 0.0).astype(jnp.bfloat16))
-            a = jnp.concatenate(a, axis=1).astype(jnp.bfloat16)
-            tally_ref[i * 8 + j] = nt_dot(a, jnp.concatenate(b, axis=1))
+                low = rows16(lo[p, j:j + 1])
+                a.append(jnp.where(rows16(hi[p, j:j + 1]) == hi_ids, rows16(weight[p, j:j + 1]), zero))
+                b.append(jnp.concatenate([jnp.where(low == ids, one, zero) for ids in lo_ids], axis=0))
+            table = nt_dot(jnp.concatenate(a, axis=1), jnp.concatenate(b, axis=1))
+            tally_ref[i * 8 + j] = jnp.concatenate([table[:8], table[8:]], axis=1)
         return 0
 
     lax.fori_loop(0, cells // 8, step, 0)

time: 116 us -> 94.5 us (0.81)
  Pallas kernels: 108 us -> 86.6 us
    pallas_call x1, Pallas kernels: 73.8 us -> 60.9 us  [compact(): pl.pallas_call(functools.partial(compact_kernel, n_rows, tree_count), out...]
    pallas_call x1, Pallas kernels: 20.7 us -> 13.2 us  [tally(): pl.pallas_call(functools.partial(tally_kernel, leaf_block), out_shape=[ja...]
where the time goes in v3:
time: 94.5 us; the launch traced here: 94.2 us
  Pallas kernels  86.6 us (92%)
  local copies, waits for them, and re-layouts  6.89 us (7%)
    pallas_call x1, Pallas kernels, compact(): pl.pallas_call(functools.partial(compact_kernel, n_rows, tree_count), out...  60.9 us
    pallas_call x1, Pallas kernels, tally(): pl.pallas_call(functools.partial(tally_kernel, leaf_block), out_shape=[ja...  13.2 us
    pallas_call x1, Pallas kernels, rates(): pl.pallas_call(functools.partial(rates_kernel, n_rows, tree_count), out_s...  12.6 us
    unnamed x9, local copies, waits for them, and re-layouts  3.55 us

profile of v3, /device:TPU:0, one launch (start us, length us, event | category | flops | bytes accessed | tf_op | source)
XLA Modules:
  0.0 94.2 jit_solution(8615420877252085844)
XLA Ops:
  0.6 0.0 copy-start
  0.6 1.2 %copy-done = s32[128,2048]{1,0:T(8,128)S(1)} copy-done((s32[128,2048]{1,0:T(8,128)S(1)}, s32[128,2048]{1,0:T(8,128)}, u32[]{:S(2)}) %copy-start) | copy-done | bytes 1048600
  1.9 0.0 copy-start.1
  1.9 1.0 %copy-done.1 = bf16[128,2048]{1,0:T(8,128)(2,1)S(1)} copy-done((bf16[128,2048]{1,0:T(8,128)(2,1)S(1)}, bf16[128,2048]{1,0:T(8,128)(2,1)}, u32[]{:S(2)}) %copy-start.1) | copy-done | bytes 524312
  2.9 0.0 copy-start.2
  2.9 0.7 copy-done.2
  3.6 60.9 %compact.1.recv_ref = f32[32,128,128]{2,1,0:T(8,128)S(1)} custom-call(s32[128,2048]{1,0:T(8,128)S(1)} %copy-done, bf16[128,2048]{1,0:T(8,128)(2,1)S(1)} %copy-done.1, s32[1,2048]{1,0:T(1,128)S(1)} %bitcast.10), custom_call_target="tpu_custom_call" | custom-call | tf_op jit(solution)/shard_map/compact/pallas_call | solution.py:156
  64.5 13.2 %tally.1 = (f32[128,8,128]{2,1,0:T(8,128)S(1)}, f32[8,128]{1,0:T(8,128)S(1)}) custom-call(f32[32,128,128]{2,1,0:T(8,128)S(1)} %compact.1.recv_ref), custom_call_target="tpu_custom_call" | custom-call | tf_op jit(solution)/shard_map/tally/pallas_call | solution.py:276
  77.7 0.0 copy-start.3
  77.7 0.1 copy.8
  77.8 0.5 copy-done.3
  78.3 0.9 %reshape.17 = f32[32,4,1000]{2,1,0:T(4,128)} reshape(f32[128,1000]{1,0:T(8,128)S(1)} %bitcast.11) | data formatting | bytes 1024000 | tf_op jit(solution)/shard_map/reshape | solution.py:298
  79.2 12.6 %rates.1 = f32[8,128]{1,0:T(8,128)} custom-call(f32[8,128]{1,0:T(8,128)} %copy-done.3), custom_call_target="tpu_custom_call" | custom-call | tf_op jit(solution)/shard_map/rates/pallas_call | solution.py:216
  91.8 1.2 %slice.11 = f32[1,1]{1,0:T(1,128)} slice(f32[8,128]{1,0:T(8,128)} %rates.1), slice={[1:2], [0:1]} | slice | bytes 8 | tf_op jit(solution)/shard_map/slice | solution.py:300
  93.0 1.2 %slice_bitcast_fusion = f32[32]{0:T(128)} fusion(f32[8,128]{1,0:T(8,128)} %rates.1), kind=kLoop, calls=%fused_computation.1 | loop fusion | bytes 256 | tf_op jit(solution)/shard_map/squeeze | solution.py:300
Async XLA Ops:
  0.6 1.2 %copy-start = (s32[128,2048]{1,0:T(8,128)S(1)}, s32[128,2048]{1,0:T(8,128)}, u32[]{:S(2)}) copy-start(s32[128,2048]{1,0:T(8,128)} %leaf_ref.1) | copy-start | bytes 3145732
  1.9 1.0 %copy-start.1 = (bf16[128,2048]{1,0:T(8,128)(2,1)S(1)}, bf16[128,2048]{1,0:T(8,128)(2,1)}, u32[]{:S(2)}) copy-start(bf16[128,2048]{1,0:T(8,128)(2,1)} %bag_ref.1) | copy-start | bytes 1572868
  2.9 0.7 copy-start.2
  77.7 0.6 copy-start.3

commit v4 on v0

v4 whole, which is shorter than its diff:
```python
import functools

import jax
import jax.numpy as jnp
from jax import lax
from jax.experimental import pallas as pl
from jax.experimental.pallas import tpu as pltpu
from jax.sharding import PartitionSpec as P

CLASSES = 1000
LEAVES = 32
LANES = 128
CHUNK = 256
GROUP = 4


def nt_dot(a, b):
    return lax.dot_general(a, b, (((1,), (1,)), ((), ())), preferred_element_type=jnp.float32)


def rows16(row):
    return jnp.broadcast_to(row, (16, row.shape[1])).astype(jnp.bfloat16)


def ids16(first, width):
    return (lax.broadcasted_iota(jnp.int32, (16, width), 0) + first).astype(jnp.float32).astype(jnp.bfloat16)


def compact_group(group, leaf_ref, weight_ref, hi_ref, lo_ref, tri_ref, mask_ref, hot_ref, placed_ref, first, slots):
    rows = leaf_ref.shape[1]
    chunks = rows // CHUNK
    one, zero = jnp.ones((), jnp.bfloat16), jnp.zeros((), jnp.bfloat16)
    leaf_ids = [ids16(q * 16, CHUNK) for q in range(LEAVES // 16)]
    slot_ids = [ids16(q * 16, CHUNK) for q in range(slots // 16)]
    leaf_ids32 = lax.broadcasted_iota(jnp.int32, (LEAVES, CHUNK), 0)
    for j in range(group):
        for c in range(chunks):
            cols = slice(c * CHUNK, (c + 1) * CHUNK)
            leaf = rows16(leaf_ref[pl.ds(first + j, 1), cols].astype(jnp.float32))
            weight = rows16(weight_ref[pl.ds(first + j, 1), cols])
            for q in range(LEAVES // 16):
                mask = leaf == leaf_ids[q]
                at = (j * chunks + c) * LEAVES + q * 16
                mask_ref[at:at + 16, :] = jnp.where(mask, one, zero)
                at = j * 3 * LEAVES + q * 16
                placed_ref[at:at + 16, cols] = jnp.where(mask, weight, zero)
                placed_ref[at + LEAVES:at + LEAVES + 16, cols] = jnp.where(mask, hi_ref[:, cols], zero)
                placed_ref[at + 2 * LEAVES:at + 2 * LEAVES + 16, cols] = jnp.where(mask, lo_ref[:, cols], zero)
    counts = jnp.dot(mask_ref[...], tri_ref[...], preferred_element_type=jnp.float32)
    for j in range(group):
        carry = jnp.zeros((LEAVES, 1), jnp.float32)
        for c in range(chunks):
            cols = slice(c * CHUNK, (c + 1) * CHUNK)
            at = (j * chunks + c) * LEAVES
            running = counts[at:at + LEAVES] + carry
            carry = running[:, CHUNK - 1:]
            mask = leaf_ref[pl.ds(first + j, 1), cols] == leaf_ids32
            rank = rows16(jnp.sum(jnp.where(mask, running, 0.0), axis=0, keepdims=True) - 1.0)
            for q in range(slots // 16):
                at = j * slots + q * 16
                hot_ref[at:at + 16, cols] = jnp.where(rank == slot_ids[q], one, zero)
    out = nt_dot(placed_ref[...], hot_ref[...])
    parts = []
    for j in range(group):
        mine = out[j * 3 * LEAVES:(j + 1) * 3 * LEAVES, j * slots:(j + 1) * slots]
        classes = mine[LEAVES:2 * LEAVES] + mine[2 * LEAVES:]
        parts.append(jnp.concatenate([mine[:LEAVES], classes], axis=1))
    return parts


def others(n, me, body):
    lax.fori_loop(1, n, lambda k, _: body(lax.rem(me + k, n)) or 0, 0)


def greet_all(n, tree_count, me):
    barrier = pltpu.get_barrier_semaphore()

    def greet(other):
        pl.semaphore_signal(
            barrier, inc=1, device_id=(other // tree_count, lax.rem(other, tree_count)),
            device_id_type=pl.DeviceIdType.MESH,
        )

    others(n, me, greet)
    return lambda: pl.semaphore_wait(barrier, n - 1)


def add_batch(recv_ref, tally_ref, index_of, sources):
    cells = recv_ref.shape[1]
    pairs = sources // 2
    half = LANES // 2
    low_half = lax.broadcasted_iota(jnp.int32, (8, LANES), 1) < half
    lo_ids = [ids16(q * 16, LANES) for q in range(half // 16)]
    hi_ids = ids16(0, LANES)
    one, zero = jnp.ones((), jnp.bfloat16), jnp.zeros((), jnp.bfloat16)

    def step(i, _):
        at = pl.ds(pl.multiple_of(i * 8, 8), 8)
        weights, los, his = [], [], []
        for p in range(pairs):
            first, second = recv_ref[index_of(2 * p), at, :], recv_ref[index_of(2 * p + 1), at, :]
            weights.append(jnp.where(low_half, first, pltpu.roll(second, half, 1)))
            label = jnp.where(low_half, pltpu.roll(first, half, 1), second).astype(jnp.int32)
            los.append((label & (half - 1)).astype(jnp.float32))
            his.append(((label >> 7) + ((label >> 6) & 1) * 8).astype(jnp.float32))
        for j in range(8):
            a, b = [], []
            for p in range(pairs):
                low = rows16(los[p][j:j + 1])
                a.append(jnp.where(rows16(his[p][j:j + 1]) == hi_ids, rows16(weights[p][j:j + 1]), zero))
                b.append(jnp.concatenate([jnp.where(low == ids, one, zero) for ids in lo_ids], axis=0))
            table = nt_dot(jnp.concatenate(a, axis=1), jnp.concatenate(b, axis=1))
            tally_ref[i * 8 + j] += jnp.concatenate([table[:8], table[8:]], axis=1)
        return 0

    lax.fori_loop(0, cells // 8, step, 0)


def forest_kernel(n_rows, tree_count, leaf_ref, bag_ref, label_ref, tally_ref, tree_ref, forest_ref,
                  send_ref, recv_ref, sums_ref, all_sums_ref, weight_ref, hi_ref, lo_ref, tri_ref,
                  mask_a, hot_a, placed_a, mask_b, hot_b, placed_b,
                  send_sem, recv_sem, own_sem, sums_send_sem, sums_recv_sem):
    trees, rows = leaf_ref.shape
    slots = rows // LEAVES
    leaf_block = LEAVES // n_rows
    tree_block = trees // tree_count
    cells = tree_block * leaf_block
    size = 2 * GROUP * leaf_block
    n = n_rows * tree_count
    my_row, my_tree = lax.axis_index("rows"), lax.axis_index("trees")
    me = my_row * tree_count + my_tree
    wait_all = greet_all(n, tree_count, me)

    labels = label_ref[...]
    hi = (labels >> 5) << 5
    hi_ref[...] = rows16(hi.astype(jnp.float32))
    lo_ref[...] = rows16((labels - hi).astype(jnp.float32))
    r = lax.broadcasted_iota(jnp.int32, (CHUNK, CHUNK), 0)
    c = lax.broadcasted_iota(jnp.int32, (CHUNK, CHUNK), 1)
    tri_ref[...] = jnp.where(r <= c, 1.0, 0.0).astype(jnp.bfloat16)
    weight_ref[...] = bag_ref[...].astype(jnp.float32)
    tally_ref[...] = jnp.zeros_like(tally_ref)
    wait_all()

    def remote(src, dst, sender, receiver, other):
        return pltpu.make_async_remote_copy(
            src_ref=src, dst_ref=dst, send_sem=sender, recv_sem=receiver,
            device_id=(other // tree_count, lax.rem(other, tree_count)),
            device_id_type=pl.DeviceIdType.MESH,
        )

    def piece(i, tt):
        first = tt * tree_block + i * 2 * GROUP
        parts = compact_group(GROUP, leaf_ref, weight_ref, hi_ref, lo_ref, tri_ref,
                              mask_a, hot_a, placed_a, first, slots)
        parts += compact_group(GROUP, leaf_ref, weight_ref, hi_ref, lo_ref, tri_ref,
                               mask_b, hot_b, placed_b, first + GROUP, slots)
        at = pl.ds(pl.multiple_of(i * size, size), size)
        for b in range(n_rows):
            tile = jnp.concatenate([p[b * leaf_block:(b + 1) * leaf_block] for p in parts], axis=0)
            send_ref[b * tree_count + tt, at, :] = tile

        def send(k, _):
            other = lax.rem(my_row + k, n_rows) * tree_count + tt

            @pl.when(other != me)
            def _():
                remote(send_ref.at[other, at], recv_ref.at[me, at], send_sem.at[other], recv_sem.at[me], other).start()

            return 0

        lax.fori_loop(0, n_rows, send, 0)

    def whole(other):
        return remote(send_ref.at[other], recv_ref.at[other], send_sem.at[other], recv_sem.at[other], other)

    own = pltpu.make_async_copy(send_ref.at[me], recv_ref.at[me], own_sem)

    def phase(i, _):
        @pl.when(i < tree_count)
        def _():
            tt = lax.rem(my_tree + i + 1, tree_count)
            lax.fori_loop(0, tree_block // (2 * GROUP), lambda j, _: piece(j, tt) or 0, 0)

        @pl.when(i == tree_count - 1)
        def _():
            own.start()

        @pl.when(i > 0)
        def _():
            sender = lax.rem(my_tree + tree_count - i, tree_count)

            def arrive(row, _):
                other = row * tree_count + sender
                pl.when(other != me)(lambda: whole(other).wait_recv())
                return 0

            lax.fori_loop(0, n_rows, arrive, 0)
            pl.when(i == tree_count)(own.wait)
            add_batch(recv_ref, tally_ref, lambda row: row * tree_count + sender, n_rows)

        return 0

    lax.fori_loop(0, tree_count + 1, phase, 0)

    table = tally_ref[...]
    seen = jnp.sum(jnp.sum(table, axis=1), axis=1, keepdims=True)
    top = jnp.max(jnp.max(table, axis=1), axis=1, keepdims=True)
    tree = lax.broadcasted_iota(jnp.int32, (cells, LANES), 0) // leaf_block
    held = tree == lax.broadcasted_iota(jnp.int32, (cells, LANES), 1)
    sums_ref[...] = jnp.zeros((8, LANES), jnp.float32)
    sums_ref[0:1] = jnp.sum(jnp.where(held, seen - top, 0.0), axis=0, keepdims=True)
    sums_ref[1:2] = jnp.sum(jnp.where(held, seen, 0.0), axis=0, keepdims=True)

    def sums_copy(slot, other):
        return remote(sums_ref, all_sums_ref.at[slot], sums_send_sem.at[other], sums_recv_sem.at[slot], other)

    others(n, me, lambda other: sums_copy(me, other).start())
    all_sums_ref[me] = sums_ref[...]
    others(n, me, lambda other: whole(other).wait_send())
    others(n, me, lambda other: sums_copy(other, other).wait())
    mine = jnp.zeros((8, LANES), jnp.float32)
    total = jnp.zeros((8, LANES), jnp.float32)
    for row in range(n_rows):
        mine += all_sums_ref[row * tree_count + my_tree]
    for device in range(n):
        total += all_sums_ref[device]
    pooled = jnp.sum(total, axis=1, keepdims=True)
    tree_ref[...] = mine[0:1, :tree_block] / mine[1:2, :tree_block]
    forest_ref[...] = pooled[0:1] / pooled[1:2]


def forest(leaf_index, out_of_bag, labels, n_rows, tree_count):
    trees, rows = leaf_index.shape
    n = n_rows * tree_count
    tree_block = trees // tree_count
    cells = tree_block * (LEAVES // n_rows)
    vmem = pl.BlockSpec(memory_space=pltpu.VMEM)
    group_scratch = [
        pltpu.VMEM((GROUP * LEAVES * (rows // CHUNK), CHUNK), jnp.bfloat16),
        pltpu.VMEM((GROUP * (rows // LEAVES), rows), jnp.bfloat16),
        pltpu.VMEM((GROUP * 3 * LEAVES, rows), jnp.bfloat16),
    ]
    return pl.pallas_call(
        functools.partial(forest_kernel, n_rows, tree_count),
        out_shape=[
            jax.ShapeDtypeStruct((cells, pl.cdiv(CLASSES, LANES), LANES), jnp.float32),
            jax.ShapeDtypeStruct((1, tree_block), jnp.float32),
            jax.ShapeDtypeStruct((1, 1), jnp.float32),
        ],
        in_specs=[vmem] * 3,
        out_specs=[vmem] * 3,
        scratch_shapes=[
            pltpu.VMEM((n, cells, LANES), jnp.float32),
            pltpu.VMEM((n, cells, LANES), jnp.float32),
            pltpu.VMEM((8, LANES), jnp.float32),
            pltpu.VMEM((n, 8, LANES), jnp.float32),
            pltpu.VMEM((trees, rows), jnp.float32),
            pltpu.VMEM((16, rows), jnp.bfloat16),
            pltpu.VMEM((16, rows), jnp.bfloat16),
            pltpu.VMEM((CHUNK, CHUNK), jnp.bfloat16),
            *group_scratch,
            *group_scratch,
            pltpu.SemaphoreType.DMA((n,)),
            pltpu.SemaphoreType.DMA((n,)),
            pltpu.SemaphoreType.DMA,
            pltpu.SemaphoreType.DMA((n,)),
            pltpu.SemaphoreType.DMA((n,)),
        ],
        compiler_params=pltpu.CompilerParams(
            vmem_limit_bytes=48 << 20, collective_id=0, has_side_effects=True
        ),
        name="forest",
    )(leaf_index, out_of_bag, labels.reshape(1, rows))


def per_device(leaf_index, out_of_bag, labels):
    n_rows = lax.axis_size("rows")
    tree_count = lax.axis_size("trees")
    trees = leaf_index.shape[0]
    tree_block = trees // tree_count
    leaf_block = LEAVES // n_rows
    cells = tree_block * leaf_block
    table, tree_error, pooled = forest(leaf_index, out_of_bag, labels, n_rows, tree_count)
    tallies = table.reshape(cells, -1)[:, :CLASSES].reshape(tree_block, leaf_block, CLASSES)
    return tallies, tree_error.reshape(tree_block), pooled.reshape(())


def solution(mesh):
    in_specs = (P(None, ("rows", "trees")), P(None, ("rows", "trees")), P(("rows", "trees")))
    out_specs = (P("trees", "rows", None), P("trees"), P())
    return jax.shard_map(
        per_device, mesh=mesh, in_specs=in_specs, out_specs=out_specs, check_vma=False
    )
```

time: 297 us -> 81.8 us (0.28)
  waiting for transfers between devices: 186 us -> 0 us
  Pallas kernels: 0 us -> 74.6 us
  local copies, waits for them, and re-layouts: 41.6 us -> 4.51 us
  blocking collectives: 27.7 us -> 0 us
  matrix products: 21.7 us -> 0 us
  between operations: 16.5 us -> 2.39 us
    reduce_scatter x1 -> x0, waiting for transfers between devices: 186 us -> none  [per_device(): lax.psum_scatter(ordered, ('rows', 'trees'), scatter_dimension=0, tiled=T...]
    pallas_call x0 -> x1, Pallas kernels: none -> 74.6 us  [forest(): pl.pallas_call(functools.partial(forest_kernel, n_rows, tree_count), out_...]
    psum x2 -> x0, blocking collectives: 27.7 us -> none  [the longest x1 20.1 us: per_device(): wrong_sum, seen_sum = lax.psum((local_wrong, local_seen), 'rows')]
    dot_general x1 -> x0, matrix products: 21.7 us -> none  [count_table(): jnp.einsum('rtlz,zc->rtlc', placed, class_onehot, preferred_element_type=...]
    reshape x2 -> x1, local copies, waits for them, and re-layouts: 21.5 us -> 0.95 us  [per_device(): table.reshape(cells, -1)[:, :CLASSES]]
    dot_general x1 -> x0, local copies, waits for them, and re-layouts: 19.9 us -> none  [count_table(): jnp.einsum('rtlz,zc->rtlc', placed, class_onehot, preferred_element_type=...]
    unnamed x0 -> x8, local copies, waits for them, and re-layouts: none -> 3.56 us
  transfers between devices with their start and end apart: 1 -> 0, of which waited for: 1 -> 0; matrix products, arithmetic and copies ran while one was open for 0% -> 0% of each run, Pallas kernels for 0% -> 0%
where the time goes in v4:
time: 81.8 us; the launch traced here: 81.5 us
  Pallas kernels  74.6 us (91%)
  local copies, waits for them, and re-layouts  4.51 us (6%)
  between operations  2.39 us (3%)
    pallas_call x1, Pallas kernels, forest(): pl.pallas_call(functools.partial(forest_kernel, n_rows, tree_count), out_...  74.6 us
    unnamed x8, local copies, waits for them, and re-layouts  3.56 us

profile of v4, /device:TPU:0, one launch (start us, length us, event | category | flops | bytes accessed | tf_op | source)
XLA Modules:
  0.0 81.5 jit_solution(6269126575297287317)
XLA Ops:
  0.6 0.0 copy-start
  0.6 1.2 %copy-done = s32[128,2048]{1,0:T(8,128)S(1)} copy-done((s32[128,2048]{1,0:T(8,128)S(1)}, s32[128,2048]{1,0:T(8,128)}, u32[]{:S(2)}) %copy-start) | copy-done | bytes 1048600
  1.9 0.0 copy-start.1
  1.9 1.0 %copy-done.1 = bf16[128,2048]{1,0:T(8,128)(2,1)S(1)} copy-done((bf16[128,2048]{1,0:T(8,128)(2,1)S(1)}, bf16[128,2048]{1,0:T(8,128)(2,1)}, u32[]{:S(2)}) %copy-start.1) | copy-done | bytes 524312
  2.9 0.0 copy-start.2
  2.9 0.7 copy-done.2
  3.6 74.6 %forest.1 = (f32[128,8,128]{2,1,0:T(8,128)S(1)}, f32[1,32]{1,0:T(1,128)S(1)}, f32[1,1]{1,0:T(1,128)}) custom-call(s32[128,2048]{1,0:T(8,128)S(1)} %copy-done, bf16[128,2048]{1,0:T(8,128)(2,1)S(1)} %copy-done.1, s32[1,2048]{1,0:T(1,128)S(1)} %bitcast.9), custom_call_target="tpu_custom_call" | custom-call | tf_op jit(solution)/shard_map/forest/pallas_call | solution.py:244
  78.2 0.1 copy.8
  78.3 0.9 %reshape.23 = f32[32,4,1000]{2,1,0:T(4,128)} reshape(f32[128,1000]{1,0:T(8,128)S(1)} %bitcast.11) | data formatting | bytes 1024000 | tf_op jit(solution)/shard_map/reshape | solution.py:285
  79.3 0.5 copy.11
Async XLA Ops:
  0.6 1.2 %copy-start = (s32[128,2048]{1,0:T(8,128)S(1)}, s32[128,2048]{1,0:T(8,128)}, u32[]{:S(2)}) copy-start(s32[128,2048]{1,0:T(8,128)} %leaf_ref.1) | copy-start | bytes 3145732
  1.9 1.0 %copy-start.1 = (bf16[128,2048]{1,0:T(8,128)(2,1)S(1)}, bf16[128,2048]{1,0:T(8,128)(2,1)}, u32[]{:S(2)}) copy-start(bf16[128,2048]{1,0:T(8,128)(2,1)} %bag_ref.1) | copy-start | bytes 1572868
  2.9 0.7 copy-start.2

commit v5 on v4

--- a/solution.py
+++ b/solution.py
@@ -12,6 +12,7 @@
 LANES = 128
 CHUNK = 256
 GROUP = 4
+COUNT_STEP = 128.0
 
 
 def nt_dot(a, b):
@@ -26,45 +27,52 @@
     return (lax.broadcasted_iota(jnp.int32, (16, width), 0) + first).astype(jnp.float32).astype(jnp.bfloat16)
 
 
-def compact_group(group, leaf_ref, weight_ref, hi_ref, lo_ref, tri_ref, mask_ref, hot_ref, placed_ref, first, slots):
+def compact_group(group, leaf_ref, weight_ref, code_ref, tri_ref, mask_ref, hot_ref, placed_ref, first, slots):
     rows = leaf_ref.shape[1]
     chunks = rows // CHUNK
     one, zero = jnp.ones((), jnp.bfloat16), jnp.zeros((), jnp.bfloat16)
+    second = jnp.full((), COUNT_STEP, jnp.bfloat16)
     leaf_ids = [ids16(q * 16, CHUNK) for q in range(LEAVES // 16)]
     slot_ids = [ids16(q * 16, CHUNK) for q in range(slots // 16)]
     leaf_ids32 = lax.broadcasted_iota(jnp.int32, (LEAVES, CHUNK), 0)
-    for j in range(group):
+    for pair in range(group // 2):
         for c in range(chunks):
             cols = slice(c * CHUNK, (c + 1) * CHUNK)
-            leaf = rows16(leaf_ref[pl.ds(first + j, 1), cols].astype(jnp.float32))
-            weight = rows16(weight_ref[pl.ds(first + j, 1), cols])
+            code = code_ref[:, cols]
+            masks = []
+            for j in (2 * pair, 2 * pair + 1):
+                leaf = rows16(leaf_ref[pl.ds(first + j, 1), cols].astype(jnp.float32))
+                weight = rows16(weight_ref[pl.ds(first + j, 1), cols])
+                masks.append([leaf == ids for ids in leaf_ids])
+                for q, mask in enumerate(masks[-1]):
+                    at = j * 2 * LEAVES + q * 16
+                    placed_ref[at:at + 16, cols] = jnp.where(mask, weight, zero)
+                    placed_ref[at + LEAVES:at + LEAVES + 16, cols] = jnp.where(mask, code, zero)
             for q in range(LEAVES // 16):
-                mask = leaf == leaf_ids[q]
-                at = (j * chunks + c) * LEAVES + q * 16
-                mask_ref[at:at + 16, :] = jnp.where(mask, one, zero)
-                at = j * 3 * LEAVES + q * 16
-                placed_ref[at:at + 16, cols] = jnp.where(mask, weight, zero)
-                placed_ref[at + LEAVES:at + LEAVES + 16, cols] = jnp.where(mask, hi_ref[:, cols], zero)
-                placed_ref[at + 2 * LEAVES:at + 2 * LEAVES + 16, cols] = jnp.where(mask, lo_ref[:, cols], zero)
+                at = (pair * chunks + c) * LEAVES + q * 16
+                mask_ref[at:at + 16, :] = jnp.where(masks[0][q], one, zero) + jnp.where(masks[1][q], second, zero)
     counts = jnp.dot(mask_ref[...], tri_ref[...], preferred_element_type=jnp.float32)
-    for j in range(group):
+    for pair in range(group // 2):
         carry = jnp.zeros((LEAVES, 1), jnp.float32)
         for c in range(chunks):
             cols = slice(c * CHUNK, (c + 1) * CHUNK)
-            at = (j * chunks + c) * LEAVES
+            at = (pair * chunks + c) * LEAVES
             running = counts[at:at + LEAVES] + carry
             carry = running[:, CHUNK - 1:]
-            mask = leaf_ref[pl.ds(first + j, 1), cols] == leaf_ids32
-            rank = rows16(jnp.sum(jnp.where(mask, running, 0.0), axis=0, keepdims=True) - 1.0)
-            for q in range(slots // 16):
-                at = j * slots + q * 16
-                hot_ref[at:at + 16, cols] = jnp.where(rank == slot_ids[q], one, zero)
+            for side in range(2):
+                j = 2 * pair + side
+                mask = leaf_ref[pl.ds(first + j, 1), cols] == leaf_ids32
+                both = jnp.sum(jnp.where(mask, running, 0.0), axis=0, keepdims=True)
+                high = jnp.floor(both * (1.0 / COUNT_STEP))
+                rank = rows16((high if side else both - high * COUNT_STEP) - 1.0)
+                for q in range(slots // 16):
+                    at_slot = j * slots + q * 16
+                    hot_ref[at_slot:at_slot + 16, cols] = jnp.where(rank == slot_ids[q], one, zero)
     out = nt_dot(placed_ref[...], hot_ref[...])
     parts = []
     for j in range(group):
-        mine = out[j * 3 * LEAVES:(j + 1) * 3 * LEAVES, j * slots:(j + 1) * slots]
-        classes = mine[LEAVES:2 * LEAVES] + mine[2 * LEAVES:]
-        parts.append(jnp.concatenate([mine[:LEAVES], classes], axis=1))
+        mine = out[j * 2 * LEAVES:(j + 1) * 2 * LEAVES, j * slots:(j + 1) * slots]
+        parts.append(jnp.concatenate([mine[:LEAVES], mine[LEAVES:]], axis=1))
     return parts
 
 
@@ -100,9 +108,13 @@
         for p in range(pairs):
             first, second = recv_ref[index_of(2 * p), at, :], recv_ref[index_of(2 * p + 1), at, :]
             weights.append(jnp.where(low_half, first, pltpu.roll(second, half, 1)))
-            label = jnp.where(low_half, pltpu.roll(first, half, 1), second).astype(jnp.int32)
-            los.append((label & (half - 1)).astype(jnp.float32))
-            his.append(((label >> 7) + ((label >> 6) & 1) * 8).astype(jnp.float32))
+            code = jnp.where(low_half, pltpu.roll(first, half, 1), second)
+            power = jnp.zeros((8, LANES), jnp.int32)
+            for k in range(1, -(-CLASSES // LANES)):
+                power += jnp.where(code >= float(LANES << k), 1, 0)
+            low = (code.astype(jnp.int32) >> power) & (LANES - 1)
+            los.append((low & (half - 1)).astype(jnp.float32))
+            his.append((power + (low >> 6) * 8).astype(jnp.float32))
         for j in range(8):
             a, b = [], []
             for p in range(pairs):
@@ -117,7 +129,7 @@
 
 
 def forest_kernel(n_rows, tree_count, leaf_ref, bag_ref, label_ref, tally_ref, tree_ref, forest_ref,
-                  send_ref, recv_ref, sums_ref, all_sums_ref, weight_ref, hi_ref, lo_ref, tri_ref,
+                  send_ref, recv_ref, sums_ref, all_sums_ref, weight_ref, code_ref, tri_ref,
                   mask_a, hot_a, placed_a, mask_b, hot_b, placed_b,
                   send_sem, recv_sem, own_sem, sums_send_sem, sums_recv_sem):
     trees, rows = leaf_ref.shape
@@ -132,9 +144,7 @@
     wait_all = greet_all(n, tree_count, me)
 
     labels = label_ref[...]
-    hi = (labels >> 5) << 5
-    hi_ref[...] = rows16(hi.astype(jnp.float32))
-    lo_ref[...] = rows16((labels - hi).astype(jnp.float32))
+    code_ref[...] = rows16(((labels % LANES + LANES) << (labels // LANES)).astype(jnp.float32))
     r = lax.broadcasted_iota(jnp.int32, (CHUNK, CHUNK), 0)
     c = lax.broadcasted_iota(jnp.int32, (CHUNK, CHUNK), 1)
     tri_ref[...] = jnp.where(r <= c, 1.0, 0.0).astype(jnp.bfloat16)
@@ -151,9 +161,9 @@
 
     def piece(i, tt):
         first = tt * tree_block + i * 2 * GROUP
-        parts = compact_group(GROUP, leaf_ref, weight_ref, hi_ref, lo_ref, tri_ref,
+        parts = compact_group(GROUP, leaf_ref, weight_ref, code_ref, tri_ref,
                               mask_a, hot_a, placed_a, first, slots)
-        parts += compact_group(GROUP, leaf_ref, weight_ref, hi_ref, lo_ref, tri_ref,
+        parts += compact_group(GROUP, leaf_ref, weight_ref, code_ref, tri_ref,
                                mask_b, hot_b, placed_b, first + GROUP, slots)
         at = pl.ds(pl.multiple_of(i * size, size), size)
         for b in range(n_rows):
@@ -237,9 +247,9 @@
     cells = tree_block * (LEAVES // n_rows)
     vmem = pl.BlockSpec(memory_space=pltpu.VMEM)
     group_scratch = [
-        pltpu.VMEM((GROUP * LEAVES * (rows // CHUNK), CHUNK), jnp.bfloat16),
+        pltpu.VMEM((GROUP // 2 * LEAVES * (rows // CHUNK), CHUNK), jnp.bfloat16),
         pltpu.VMEM((GROUP * (rows // LEAVES), rows), jnp.bfloat16),
-        pltpu.VMEM((GROUP * 3 * LEAVES, rows), jnp.bfloat16),
+        pltpu.VMEM((GROUP * 2 * LEAVES, rows), jnp.bfloat16),
     ]
     return pl.pallas_call(
         functools.partial(forest_kernel, n_rows, tree_count),
@@ -257,7 +267,6 @@
             pltpu.VMEM((n, 8, LANES), jnp.float32),
             pltpu.VMEM((trees, rows), jnp.float32),
             pltpu.VMEM((16, rows), jnp.bfloat16),
-            pltpu.VMEM((16, rows), jnp.bfloat16),
             pltpu.VMEM((CHUNK, CHUNK), jnp.bfloat16),
             *group_scratch,
             *group_scratch,

time: 81.8 us -> 80.9 us (0.989)
  Pallas kernels: 74.6 us -> 73.7 us
    pallas_call x1, Pallas kernels: 74.6 us -> 73.7 us  [forest(): pl.pallas_call(functools.partial(forest_kernel, n_rows, tree_count), out_...]
where the time goes in v5:
time: 80.9 us; the launch traced here: 80.6 us
  Pallas kernels  73.7 us (91%)
  local copies, waits for them, and re-layouts  4.51 us (6%)
  between operations  2.39 us (3%)
    pallas_call x1, Pallas kernels, forest(): pl.pallas_call(functools.partial(forest_kernel, n_rows, tree_count), out_...  73.7 us
    unnamed x8, local copies, waits for them, and re-layouts  3.56 us

profile of v5, /device:TPU:0, one launch (start us, length us, event | category | flops | bytes accessed | tf_op | source)
XLA Modules:
  0.0 80.6 jit_solution(1798055022341371029)
XLA Ops:
  0.6 0.0 copy-start
  0.6 1.2 %copy-done = s32[128,2048]{1,0:T(8,128)S(1)} copy-done((s32[128,2048]{1,0:T(8,128)S(1)}, s32[128,2048]{1,0:T(8,128)}, u32[]{:S(2)}) %copy-start) | copy-done | bytes 1048600
  1.9 0.0 copy-start.1
  1.9 1.0 %copy-done.1 = bf16[128,2048]{1,0:T(8,128)(2,1)S(1)} copy-done((bf16[128,2048]{1,0:T(8,128)(2,1)S(1)}, bf16[128,2048]{1,0:T(8,128)(2,1)}, u32[]{:S(2)}) %copy-start.1) | copy-done | bytes 524312
  2.9 0.0 copy-start.2
  2.9 0.7 copy-done.2
  3.6 73.7 %forest.1 = (f32[128,8,128]{2,1,0:T(8,128)S(1)}, f32[1,32]{1,0:T(1,128)S(1)}, f32[1,1]{1,0:T(1,128)}) custom-call(s32[128,2048]{1,0:T(8,128)S(1)} %copy-done, bf16[128,2048]{1,0:T(8,128)(2,1)S(1)} %copy-done.1, s32[1,2048]{1,0:T(1,128)S(1)} %bitcast.9), custom_call_target="tpu_custom_call" | custom-call | tf_op jit(solution)/shard_map/forest/pallas_call | solution.py:254
  77.3 0.1 copy.8
  77.5 0.9 %reshape.23 = f32[32,4,1000]{2,1,0:T(4,128)} reshape(f32[128,1000]{1,0:T(8,128)S(1)} %bitcast.11) | data formatting | bytes 1024000 | tf_op jit(solution)/shard_map/reshape | solution.py:294
  78.4 0.5 copy.11
Async XLA Ops:
  0.6 1.2 %copy-start = (s32[128,2048]{1,0:T(8,128)S(1)}, s32[128,2048]{1,0:T(8,128)}, u32[]{:S(2)}) copy-start(s32[128,2048]{1,0:T(8,128)} %leaf_ref.1) | copy-start | bytes 3145732
  1.9 1.0 %copy-start.1 = (bf16[128,2048]{1,0:T(8,128)(2,1)S(1)}, bf16[128,2048]{1,0:T(8,128)(2,1)}, u32[]{:S(2)}) copy-start(bf16[128,2048]{1,0:T(8,128)(2,1)} %bag_ref.1) | copy-start | bytes 1572868
  2.9 0.7 copy-start.2

commit v6 on v5

--- a/solution.py
+++ b/solution.py
@@ -11,7 +11,8 @@
 LEAVES = 32
 LANES = 128
 CHUNK = 256
-GROUP = 4
+GROUP = 8
+BATCH = 4
 COUNT_STEP = 128.0
 
 
@@ -53,12 +54,13 @@
                 mask_ref[at:at + 16, :] = jnp.where(masks[0][q], one, zero) + jnp.where(masks[1][q], second, zero)
     counts = jnp.dot(mask_ref[...], tri_ref[...], preferred_element_type=jnp.float32)
     for pair in range(group // 2):
-        carry = jnp.zeros((LEAVES, 1), jnp.float32)
+        carry = jnp.zeros((LEAVES, LANES), jnp.float32)
         for c in range(chunks):
             cols = slice(c * CHUNK, (c + 1) * CHUNK)
             at = (pair * chunks + c) * LEAVES
-            running = counts[at:at + LEAVES] + carry
-            carry = running[:, CHUNK - 1:]
+            here = counts[at:at + LEAVES]
+            running = here + jnp.concatenate([carry] * (CHUNK // LANES), axis=1)
+            carry = carry + jnp.broadcast_to(here[:, CHUNK - 1:], (LEAVES, LANES))
             for side in range(2):
                 j = 2 * pair + side
                 mask = leaf_ref[pl.ds(first + j, 1), cols] == leaf_ids32
@@ -68,11 +70,13 @@
                 for q in range(slots // 16):
                     at_slot = j * slots + q * 16
                     hot_ref[at_slot:at_slot + 16, cols] = jnp.where(rank == slot_ids[q], one, zero)
-    out = nt_dot(placed_ref[...], hot_ref[...])
     parts = []
-    for j in range(group):
-        mine = out[j * 2 * LEAVES:(j + 1) * 2 * LEAVES, j * slots:(j + 1) * slots]
-        parts.append(jnp.concatenate([mine[:LEAVES], mine[LEAVES:]], axis=1))
+    for base in range(0, group, BATCH):
+        out = nt_dot(placed_ref[base * 2 * LEAVES:(base + BATCH) * 2 * LEAVES, :],
+                     hot_ref[base * slots:(base + BATCH) * slots, :])
+        for j in range(BATCH):
+            mine = out[j * 2 * LEAVES:(j + 1) * 2 * LEAVES, j * slots:(j + 1) * slots]
+            parts.append(jnp.concatenate([mine[:LEAVES], mine[LEAVES:]], axis=1))
     return parts
 
 
@@ -128,20 +132,29 @@
     lax.fori_loop(0, cells // 8, step, 0)
 
 
-def forest_kernel(n_rows, tree_count, leaf_ref, bag_ref, label_ref, tally_ref, tree_ref, forest_ref,
+def forest_kernel(n_rows, tree_count, leaf_in, bag_in, label_in, tally_ref, tree_ref, forest_ref,
                   send_ref, recv_ref, sums_ref, all_sums_ref, weight_ref, code_ref, tri_ref,
-                  mask_a, hot_a, placed_a, mask_b, hot_b, placed_b,
+                  mask_ref, hot_ref, placed_ref, leaf_ref, bag_ref, label_ref, in_sem,
                   send_sem, recv_sem, own_sem, sums_send_sem, sums_recv_sem):
     trees, rows = leaf_ref.shape
     slots = rows // LEAVES
     leaf_block = LEAVES // n_rows
     tree_block = trees // tree_count
     cells = tree_block * leaf_block
-    size = 2 * GROUP * leaf_block
+    size = GROUP * leaf_block
     n = n_rows * tree_count
     my_row, my_tree = lax.axis_index("rows"), lax.axis_index("trees")
     me = my_row * tree_count + my_tree
+    loads = [
+        pltpu.make_async_copy(src, dst, in_sem.at[k])
+        for k, (src, dst) in enumerate([(leaf_in, leaf_ref), (bag_in, bag_ref), (label_in, label_ref)])
+    ]
+    for load in loads:
+        load.start()
     wait_all = greet_all(n, tree_count, me)
+    tally_ref[...] = jnp.zeros_like(tally_ref)
+    for load in loads:
+        load.wait()
 
     labels = label_ref[...]
     code_ref[...] = rows16(((labels % LANES + LANES) << (labels // LANES)).astype(jnp.float32))
@@ -149,7 +162,6 @@
     c = lax.broadcasted_iota(jnp.int32, (CHUNK, CHUNK), 1)
     tri_ref[...] = jnp.where(r <= c, 1.0, 0.0).astype(jnp.bfloat16)
     weight_ref[...] = bag_ref[...].astype(jnp.float32)
-    tally_ref[...] = jnp.zeros_like(tally_ref)
     wait_all()
 
     def remote(src, dst, sender, receiver, other):
@@ -160,11 +172,9 @@
         )
 
     def piece(i, tt):
-        first = tt * tree_block + i * 2 * GROUP
+        first = tt * tree_block + i * GROUP
         parts = compact_group(GROUP, leaf_ref, weight_ref, code_ref, tri_ref,
-                              mask_a, hot_a, placed_a, first, slots)
-        parts += compact_group(GROUP, leaf_ref, weight_ref, code_ref, tri_ref,
-                               mask_b, hot_b, placed_b, first + GROUP, slots)
+                              mask_ref, hot_ref, placed_ref, first, slots)
         at = pl.ds(pl.multiple_of(i * size, size), size)
         for b in range(n_rows):
             tile = jnp.concatenate([p[b * leaf_block:(b + 1) * leaf_block] for p in parts], axis=0)
@@ -190,7 +200,7 @@
         @pl.when(i < tree_count)
         def _():
             tt = lax.rem(my_tree + i + 1, tree_count)
-            lax.fori_loop(0, tree_block // (2 * GROUP), lambda j, _: piece(j, tt) or 0, 0)
+            lax.fori_loop(0, tree_block // GROUP, lambda j, _: piece(j, tt) or 0, 0)
 
         @pl.when(i == tree_count - 1)
         def _():
@@ -258,7 +268,7 @@
             jax.ShapeDtypeStruct((1, tree_block), jnp.float32),
             jax.ShapeDtypeStruct((1, 1), jnp.float32),
         ],
-        in_specs=[vmem] * 3,
+        in_specs=[pl.BlockSpec(memory_space=pltpu.HBM)] * 3,
         out_specs=[vmem] * 3,
         scratch_shapes=[
             pltpu.VMEM((n, cells, LANES), jnp.float32),
@@ -269,7 +279,10 @@
             pltpu.VMEM((16, rows), jnp.bfloat16),
             pltpu.VMEM((CHUNK, CHUNK), jnp.bfloat16),
             *group_scratch,
-            *group_scratch,
+            pltpu.VMEM((trees, rows), jnp.int32),
+            pltpu.VMEM((trees, rows), jnp.bfloat16),
+            pltpu.VMEM((1, rows), jnp.int32),
+            pltpu.SemaphoreType.DMA((3,)),
             pltpu.SemaphoreType.DMA((n,)),
             pltpu.SemaphoreType.DMA((n,)),
             pltpu.SemaphoreType.DMA,
@@ -277,7 +290,7 @@
             pltpu.SemaphoreType.DMA((n,)),
         ],
         compiler_params=pltpu.CompilerParams(
-            vmem_limit_bytes=48 << 20, collective_id=0, has_side_effects=True
+            vmem_limit_bytes=63 << 20, collective_id=0, has_side_effects=True
         ),
         name="forest",
     )(leaf_index, out_of_bag, labels.reshape(1, rows))

time: 80.9 us -> 79.8 us (0.986)
  local copies, waits for them, and re-layouts: 4.51 us -> 3.27 us
    unnamed x8 -> x4, local copies, waits for them, and re-layouts: 3.56 us -> 2.32 us
where the time goes in v6:
time: 79.8 us; the launch traced here: 79.6 us
  Pallas kernels  74 us (93%)
  local copies, waits for them, and re-layouts  3.27 us (4%)
  between operations  2.38 us (3%)
    pallas_call x1, Pallas kernels, forest(): pl.pallas_call(functools.partial(forest_kernel, n_rows, tree_count), out_...  74 us
    unnamed x4, local copies, waits for them, and re-layouts  2.32 us

profile of v6, /device:TPU:0, one launch (start us, length us, event | category | flops | bytes accessed | tf_op | source)
XLA Modules:
  0.0 79.6 jit_solution(15699798054752499002)
XLA Ops:
  0.6 74.0 %forest.1 = (f32[128,8,128]{2,1,0:T(8,128)}, f32[1,32]{1,0:T(1,128)}, f32[1,1]{1,0:T(1,128)}) custom-call(s32[128,2048]{1,0:T(8,128)} %leaf_in.1, bf16[128,2048]{1,0:T(8,128)(2,1)} %bag_in.1, s32[1,2048]{1,0:T(1,128)} %bitcast.10), custom_call_target="tpu_custom_call" | custom-call | tf_op jit(solution)/shard_map/forest/pallas_call | solution.py:264
  74.6 1.1 %copy.8 = f32[16,8,8,128]{3,1,2,0:T(8,128)S(1)} copy(f32[16,8,8,128]{3,2,1,0:T(8,128)} %bitcast.9) | data formatting | bytes 1048576
  75.7 0.9 %reshape.23 = f32[32,4,1000]{2,1,0:T(4,128)} reshape(f32[128,1000]{1,0:T(8,128)S(1)} %bitcast.8) | data formatting | bytes 1024000 | tf_op jit(solution)/shard_map/reshape | solution.py:307
  76.7 0.0 copy-start
  76.7 0.7 copy-done
  77.4 0.5 copy.11
Async XLA Ops:
  76.7 0.7 copy-start

commit v7 on v6

--- a/solution.py
+++ b/solution.py
@@ -196,32 +196,28 @@
 
     own = pltpu.make_async_copy(send_ref.at[me], recv_ref.at[me], own_sem)
 
-    def phase(i, _):
-        @pl.when(i < tree_count)
-        def _():
-            tt = lax.rem(my_tree + i + 1, tree_count)
-            lax.fori_loop(0, tree_block // GROUP, lambda j, _: piece(j, tt) or 0, 0)
-
-        @pl.when(i == tree_count - 1)
-        def _():
-            own.start()
-
-        @pl.when(i > 0)
-        def _():
-            sender = lax.rem(my_tree + tree_count - i, tree_count)
-
-            def arrive(row, _):
-                other = row * tree_count + sender
-                pl.when(other != me)(lambda: whole(other).wait_recv())
-                return 0
-
-            lax.fori_loop(0, n_rows, arrive, 0)
-            pl.when(i == tree_count)(own.wait)
-            add_batch(recv_ref, tally_ref, lambda row: row * tree_count + sender, n_rows)
-
+    def outgoing(i, _):
+        tt = lax.rem(my_tree + i + 1, tree_count)
+        lax.fori_loop(0, tree_block // GROUP, lambda j, _: piece(j, tt) or 0, 0)
         return 0
 
-    lax.fori_loop(0, tree_count + 1, phase, 0)
+    lax.fori_loop(0, tree_count, outgoing, 0)
+    own.start()
+
+    def incoming(i, _):
+        sender = lax.rem(my_tree + tree_count - i, tree_count)
+
+        def arrive(row, _):
+            other = row * tree_count + sender
+            pl.when(other != me)(lambda: whole(other).wait_recv())
+            return 0
+
+        lax.fori_loop(0, n_rows, arrive, 0)
+        pl.when(i == tree_count)(own.wait)
+        add_batch(recv_ref, tally_ref, lambda row: row * tree_count + sender, n_rows)
+        return 0
+
+    lax.fori_loop(1, tree_count + 1, incoming, 0)
 
     table = tally_ref[...]
     seen = jnp.sum(jnp.sum(table, axis=1), axis=1, keepdims=True)

time: 79.8 us -> 76.4 us (0.957)
  Pallas kernels: 74 us -> 70.6 us
    pallas_call x1, Pallas kernels: 74 us -> 70.6 us  [forest(): pl.pallas_call(functools.partial(forest_kernel, n_rows, tree_count), out_...]
where the time goes in v7:
time: 76.4 us; the launch traced here: 76.2 us
  Pallas kernels  70.6 us (92%)
  local copies, waits for them, and re-layouts  3.27 us (4%)
  between operations  2.38 us (3%)
    pallas_call x1, Pallas kernels, forest(): pl.pallas_call(functools.partial(forest_kernel, n_rows, tree_count), out_...  70.6 us
    unnamed x4, local copies, waits for them, and re-layouts  2.32 us

profile of v7, /device:TPU:0, one launch (start us, length us, event | category | flops | bytes accessed | tf_op | source)
XLA Modules:
  0.0 76.2 jit_solution(15982370117605620427)
XLA Ops:
  0.6 70.6 %forest.1 = (f32[128,8,128]{2,1,0:T(8,128)}, f32[1,32]{1,0:T(1,128)}, f32[1,1]{1,0:T(1,128)}) custom-call(s32[128,2048]{1,0:T(8,128)} %leaf_in.1, bf16[128,2048]{1,0:T(8,128)(2,1)} %bag_in.1, s32[1,2048]{1,0:T(1,128)} %bitcast.10), custom_call_target="tpu_custom_call" | custom-call | tf_op jit(solution)/shard_map/forest/pallas_call | solution.py:260
  71.2 1.1 %copy.8 = f32[16,8,8,128]{3,1,2,0:T(8,128)S(1)} copy(f32[16,8,8,128]{3,2,1,0:T(8,128)} %bitcast.9) | data formatting | bytes 1048576
  72.3 0.9 %reshape.23 = f32[32,4,1000]{2,1,0:T(4,128)} reshape(f32[128,1000]{1,0:T(8,128)S(1)} %bitcast.8) | data formatting | bytes 1024000 | tf_op jit(solution)/shard_map/reshape | solution.py:303
  73.3 0.0 copy-start
  73.3 0.7 copy-done
  74.0 0.5 copy.11
Async XLA Ops:
  73.3 0.7 copy-start

commit v8 on v7

--- a/solution.py
+++ b/solution.py
@@ -181,7 +181,7 @@
             send_ref[b * tree_count + tt, at, :] = tile
 
         def send(k, _):
-            other = lax.rem(my_row + k, n_rows) * tree_count + tt
+            other = lax.rem(my_row + n_rows // 2 + k, n_rows) * tree_count + tt
 
             @pl.when(other != me)
             def _():

time: 76.4 us -> 77 us (level)
  no operation moved by 1% of the time
where the time goes in v8:
time: 77 us; the launch traced here: 76.8 us
  Pallas kernels  71.2 us (92%)
  local copies, waits for them, and re-layouts  3.27 us (4%)
  between operations  2.38 us (3%)
    pallas_call x1, Pallas kernels, forest(): pl.pallas_call(functools.partial(forest_kernel, n_rows, tree_count), out_...  71.2 us
    unnamed x4, local copies, waits for them, and re-layouts  2.32 us

profile of v8, /device:TPU:0, one launch (start us, length us, event | category | flops | bytes accessed | tf_op | source)
XLA Modules:
  0.0 76.8 jit_solution(5749495974678106284)
XLA Ops:
  0.6 71.2 %forest.1 = (f32[128,8,128]{2,1,0:T(8,128)}, f32[1,32]{1,0:T(1,128)}, f32[1,1]{1,0:T(1,128)}) custom-call(s32[128,2048]{1,0:T(8,128)} %leaf_in.1, bf16[128,2048]{1,0:T(8,128)(2,1)} %bag_in.1, s32[1,2048]{1,0:T(1,128)} %bitcast.10), custom_call_target="tpu_custom_call" | custom-call | tf_op jit(solution)/shard_map/forest/pallas_call | solution.py:260
  71.8 1.1 %copy.8 = f32[16,8,8,128]{3,1,2,0:T(8,128)S(1)} copy(f32[16,8,8,128]{3,2,1,0:T(8,128)} %bitcast.9) | data formatting | bytes 1048576
  72.9 0.9 %reshape.23 = f32[32,4,1000]{2,1,0:T(4,128)} reshape(f32[128,1000]{1,0:T(8,128)S(1)} %bitcast.8) | data formatting | bytes 1024000 | tf_op jit(solution)/shard_map/reshape | solution.py:303
  73.9 0.0 copy-start
  73.9 0.7 copy-done
  74.6 0.5 copy.11
Async XLA Ops:
  73.9 0.7 copy-start
